TPU v7x, 512 devices: a whole 4x8x8 slice. The times are simulated.
512 devices in a mesh: row: 16 (over y, core), col: 32 (over z, x).
Axes of the slice: x: 4, y: 8, z: 8, core: 2. Of those that a mesh axis runs over, the one named last changes fastest.
Arguments:
- rhs_block: float32 [1024, 2048], P('row', 'col'), may hold values from -6 to 6
- diag_inverse: float32 [2048, 2048], P('col', 'row'), may hold values from -0.25 to 0.25
- panel: bfloat16 [2048, 196608], P(None, ('row', 'col')), may hold values from -0.125 to 0.125
- rhs_trail: float32 [1024, 196608], P(None, ('row', 'col')), may hold values from -6 to 6
Outputs:
- solved: float32 [1024, 2048], P('row', 'col')
- updated: float32 [1024, 196608], P(None, ('row', 'col'))
All inputs are finite; a program needn't handle non-finite values.
Results may differ from a plain program's by a relative error of at most 0.0022.
Values may be sent and summed in bfloat16 or wider, within the bound.
No kernel may reach another device: no remote copies, remote signals or barrier semaphores. Data moves between devices by JAX's collectives and lax.ppermute only.
A program may use at most 64 MiB of HBM per device.

v0:
```python
import jax
import jax.numpy as jnp
from jax import lax
from jax.sharding import PartitionSpec as P


def local(rhs_block, diag_inverse, panel, rhs_trail):
    inverse_band = lax.all_gather(diag_inverse, "row", axis=1, tiled=True)
    partial_value = jnp.dot(
        rhs_block, inverse_band, preferred_element_type=jnp.float32, precision=lax.Precision.HIGHEST
    )
    solved_own = lax.psum_scatter(partial_value, "col", scatter_dimension=1, tiled=True)
    solved_low = solved_own.astype(jnp.bfloat16)
    band = lax.all_gather(solved_low, "col", axis=1, tiled=True)
    update = jnp.dot(
        lax.all_gather(band, "row", axis=0, tiled=True), panel, preferred_element_type=jnp.float32
    )
    return (solved_own, rhs_trail - update)


def solution(mesh):
    return jax.shard_map(
        local,
        mesh=mesh,
        in_specs=(
            P("row", "col"),
            P("col", "row"),
            P(None, ("row", "col")),
            P(None, ("row", "col")),
        ),
        out_specs=(P("row", "col"), P(None, ("row", "col"))),
        check_vma=False,
    )
```

profile of v0, /device:TPU:1, one launch (start us, length us, event | category | flops | bytes accessed | tf_op | source)
XLA Modules:
  0.0 359.5 jit_solution(16946829252093925893)
XLA Ops:
  7.2 0.0 copy-start
  7.2 0.0 reduce-scatter.4.cloned.1.call-start
  7.2 22.8 %all_gather.9 = f32[64,2048]{1,0:T(8,128)S(1)} all-gather(f32[64,128]{1,0:T(8,128)} %param.5), channel_id=1, replica_groups=mesh['row'=16,'col'=32] {'row'}, dimensions={1}, use_global_device_ids=true | all-gather | bytes 557056 | tf_op jit(solution)/shard_map/all_gather | solution.py:8
  30.0 3.5 convolution_bitcast_fusion
  33.6 0.0 reduce-scatter.4.cloned.1.call-update
  33.6 0.0 all-gather.2.cloned.1.call-start
  33.7 214.7 %reduce-scatter.4.cloned.1.call-done = f32[64,64]{1,0:T(8,128)} async-done(((f32[2048,64]{1,0:T(8,128)}), f32[64,64]{1,0:T(8,128)}) %reduce-scatter.4.cloned.1.call-update) | async-done | bytes 16400
  248.3 0.8 copy.10
  249.2 0.0 copy-start.1
  249.2 0.1 copy.7
  249.3 36.5 %all_gather.10 = bf16[64,2048]{0,1:T(8,128)(2,1)S(1)} all-gather(bf16[64,64]{0,1:T(8,128)(2,1)S(1)} %copy.7), channel_id=1, replica_groups=mesh['row'=16,'col'=32] {'col'}, dimensions={1}, use_global_device_ids=true | all-gather | bytes 270336 | tf_op jit(solution)/shard_map/all_gather | solution.py:14
  285.8 0.9 copy.8
  286.7 0.0 all-gather.2.cloned.1.call-update
  286.7 59.8 %all-gather.2.cloned.1.call-done = bf16[1024,2048]{1,0:T(8,128)(2,1)} async-done(((bf16[64,2048]{1,0:T(8,128)(2,1)}), bf16[1024,2048]{1,0:T(8,128)(2,1)}) %all-gather.2.cloned.1.call-update) | async-done | bytes 4194320 | tf_op jit(solution)/shard_map/all_gather | solution.py:16
  346.5 0.0 copy-done
  346.5 6.1 %convolution_subtract_fusion = f32[1024,384]{1,0:T(8,128)} fusion(f32[1024,384]{1,0:T(8,128)} %param.7, bf16[1024,2048]{1,0:T(8,128)(2,1)} %all-gather.2.cloned.1.call-done, bf16[2048,384]{1,0:T(8,128)(2,1)S(1)} %copy-done), kind=kOutput, calls=%fused_computation.1 | convolution fusion | flops 1611005952 | bytes 8912896 | tf_op jit(solution)/shard_map/dot_general | solution.py:15
  352.6 0.0 copy-done.1
  (1 shorter events, 0.0 us)
Async XLA Ops:
  7.2 339.3 %copy-start = (bf16[2048,384]{1,0:T(8,128)(2,1)S(1)}, bf16[2048,384]{1,0:T(8,128)(2,1)}, u32[]{:S(2)}) copy-start(bf16[2048,384]{1,0:T(8,128)(2,1)} %param.6) | copy-start | bytes 4718596
  7.2 241.2 %reduce-scatter.4.cloned.1.call-start = ((), (), s32[]{:S(2)}) async-start(), calls=%async_computation.2 | async-start | bytes 1081344
  33.6 312.9 %all-gather.2.cloned.1.call-start = ((), (), s32[]{:S(2)}) async-start(), calls=%async_computation.1 | async-start | bytes 4456448 | tf_op jit(solution)/shard_map/all_gather | solution.py:16
  249.2 103.5 %copy-start.1 = (f32[64,64]{1,0:T(8,128)}, f32[64,64]{1,0:T(8,128)S(1)}, u32[]{:S(2)}) copy-start(f32[64,64]{1,0:T(8,128)S(1)} %copy.10) | copy-start | bytes 49156
Sparse Core Ops, SparseCore 0:
  33.7 214.5 reduce-scatter.3
  286.8 59.6 all-gather.1
where the time goes:
time: 360 us; the launch traced here: 359 us
  waiting for transfers between devices  274 us (76%)
  blocking collectives  59.3 us (16%)
  between operations  14.1 us (4%)
  matrix products  9.68 us (3%)
    unnamed x3, waiting for transfers between devices  215 us
    all_gather x1, waiting for transfers between devices, local(): lax.all_gather(band, 'row', axis=0, tiled=True)  59.8 us
    all_gather x1, blocking collectives, local(): band = lax.all_gather(solved_low, 'col', axis=1, tiled=True)  36.5 us
    all_gather x1, blocking collectives, local(): inverse_band = lax.all_gather(diag_inverse, 'row', axis=1, tiled=True)  22.8 us
  transfers between devices with their start and end apart: 2, of which 2 were waited for; matrix products, arithmetic and copies ran while one was open for 0% of the time, Pallas kernels for 0%

commit v1 on v0

v1 whole, which is shorter than its diff:
```python
import functools

import jax
import jax.numpy as jnp
from jax import lax
from jax.experimental import pallas as pl
from jax.experimental.pallas import tpu as pltpu
from jax.sharding import PartitionSpec as P


def update_kernel(blocks_ref, panel_ref, trail_ref, out_ref):
    low = jnp.concatenate([blocks_ref[i] for i in range(blocks_ref.shape[0])], axis=1)
    out_ref[...] = trail_ref[...] - jnp.dot(low, panel_ref[...], preferred_element_type=jnp.float32)


def updated_trail(blocks, panel, trail, rows=256):
    count, total, width = blocks.shape
    columns = panel.shape[1]
    return pl.pallas_call(
        update_kernel,
        out_shape=jax.ShapeDtypeStruct(trail.shape, jnp.float32),
        grid=(total // rows,),
        in_specs=[
            pl.BlockSpec((count, rows, width), lambda i: (0, i, 0)),
            pl.BlockSpec((count * width, columns), lambda i: (0, 0)),
            pl.BlockSpec((rows, columns), lambda i: (i, 0)),
        ],
        out_specs=pl.BlockSpec((rows, columns), lambda i: (i, 0)),
        compiler_params=pltpu.CompilerParams(vmem_limit_bytes=32 * 1024 * 1024),
        cost_estimate=pl.CostEstimate(
            flops=2 * total * count * width * columns, bytes_accessed=9 * 1024 * 1024, transcendentals=0
        ),
    )(blocks, panel, trail)


def placed(tile, n_row, n_col):
    odd = lax.axis_index("col") % 2 == 1
    left, right = jnp.split(tile, 2, axis=1)
    same = [(r * n_col + c, c // 2 * n_col + 2 * r + c % 2) for r in range(n_row) for c in range(n_col)]
    other = [(r * n_col + c, c // 2 * n_col + 2 * r + 1 - c % 2) for r in range(n_row) for c in range(n_col)]
    a = lax.ppermute(jnp.where(odd, right, left), ("row", "col"), same)
    b = lax.ppermute(jnp.where(odd, left, right), ("row", "col"), other)
    return jnp.where(odd, jnp.concatenate([b, a]), jnp.concatenate([a, b]))


def local(n_row, n_col, rhs_block, diag_inverse, panel, rhs_trail):
    rows = lax.all_gather(rhs_block, "row", axis=0, tiled=True)
    partial = jnp.dot(rows, diag_inverse, preferred_element_type=jnp.float32, precision=lax.Precision.HIGHEST)
    height, width = partial.shape[0] // n_col, partial.shape[1]
    shares = lax.all_to_all(partial.reshape(n_col, height, width), "col", 0, 0, tiled=True)
    tile = jnp.sum(shares, axis=0)
    low = jnp.broadcast_to(tile.astype(jnp.bfloat16)[None], (n_col, height, width))
    band = lax.all_to_all(low, "col", 0, 0, tiled=True).reshape(n_col * height, width)
    blocks = lax.all_gather(band, "row", axis=0, tiled=False)
    return placed(tile, n_row, n_col), updated_trail(blocks, panel, rhs_trail)


def solution(mesh):
    return jax.shard_map(
        functools.partial(local, mesh.shape["row"], mesh.shape["col"]),
        mesh=mesh,
        in_specs=(
            P("row", "col"),
            P("col", "row"),
            P(None, ("row", "col")),
            P(None, ("row", "col")),
        ),
        out_specs=(P("row", "col"), P(None, ("row", "col"))),
        check_vma=False,
    )
```

time: 360 us -> 128 us (0.36)
  waiting for transfers between devices: 274 us -> 31.2 us
  matrix products: 9.68 us -> 0.55 us
  starting transfers between devices: 0.08 us -> 8.51 us
  blocking collectives: 59.3 us -> 65.6 us
  Pallas kernels: 0 us -> 3.91 us
    unnamed x3 -> x1, waiting for transfers between devices: 215 us -> 0.02 us
    all_to_all x0 -> x2, blocking collectives: none -> 42.9 us  [the longest x1 27.6 us: local(): lax.all_to_all(partial.reshape(n_col, height, width), 'col', 0, 0, tiled=...]
    all_gather x2 -> x1, blocking collectives: 59.3 us -> 22.7 us  [local(): rows = lax.all_gather(rhs_block, 'row', axis=0, tiled=True)]
    all_gather x1, waiting for transfers between devices: 59.8 us -> 26.8 us  [local(): blocks = lax.all_gather(band, 'row', axis=0, tiled=False)]
    ppermute x0 -> x2, starting transfers between devices: none -> 8.47 us  [the longest x1 6.36 us: placed(): b = lax.ppermute(jnp.where(odd, left, right), ('row', 'col'), other)]
    dot_general x1, matrix products: 6.14 us -> 0.55 us  [local(): jnp.dot(rows, diag_inverse, preferred_element_type=jnp.float32, precision...]
    ppermute x0 -> x2, waiting for transfers between devices: none -> 4.44 us  [the longest x1 4.43 us: placed(): a = lax.ppermute(jnp.where(odd, right, left), ('row', 'col'), same)]
    pallas_call x0 -> x1, Pallas kernels: none -> 3.91 us  [updated_trail(): pl.pallas_call(update_kernel, out_shape=jax.ShapeDtypeStruct(trail.shape,...]
  transfers between devices with their start and end apart: 2 -> 3, of which waited for: 2 -> 2; matrix products, arithmetic and copies ran while one was open for 0% -> 1% of each run, Pallas kernels for 0% -> 0%
where the time goes in v1:
time: 128 us
  blocking collectives  65.6 us (51%)
  waiting for transfers between devices  31.2 us (24%)
  between operations  14.1 us (11%)
  starting transfers between devices  8.51 us (7%)
  Pallas kernels  3.91 us (3%)
  local copies, waits for them, and re-layouts  2.25 us (2%)
  other arithmetic  1.79 us (1%)
    all_to_all x1, blocking collectives, local(): lax.all_to_all(partial.reshape(n_col, height, width), 'col', 0, 0, tiled=...  27.6 us
    all_gather x1, waiting for transfers between devices, local(): blocks = lax.all_gather(band, 'row', axis=0, tiled=False)  26.8 us
    all_gather x1, blocking collectives, local(): rows = lax.all_gather(rhs_block, 'row', axis=0, tiled=True)  22.7 us
    all_to_all x1, blocking collectives, local(): lax.all_to_all(low, 'col', 0, 0, tiled=True).reshape(n_col * height, width)  15.3 us
    ppermute x1, starting transfers between devices, placed(): b = lax.ppermute(jnp.where(odd, left, right), ('row', 'col'), other)  6.36 us
    ppermute x1, waiting for transfers between devices, placed(): a = lax.ppermute(jnp.where(odd, right, left), ('row', 'col'), same)  4.43 us
    pallas_call x1, Pallas kernels, updated_trail(): pl.pallas_call(update_kernel, out_shape=jax.ShapeDtypeStruct(trail.shape,...  3.91 us
  transfers between devices with their start and end apart: 3, of which 2 were waited for; matrix products, arithmetic and copies ran while one was open for 1% of the time, Pallas kernels for 0%

profile of v1, /device:TPU:1, one launch (start us, length us, event | category | flops | bytes accessed | tf_op | source)
XLA Modules:
  0.0 127.9 jit_solution(6148124621877242791)
XLA Ops:
  7.2 0.0 copy-start
  7.2 0.0 all-gather.2.cloned.1.call-start
  7.2 22.7 %all_gather.6 = f32[1024,64]{1,0:T(8,128)S(1)} all-gather(f32[64,64]{1,0:T(8,128)} %param.4), channel_id=1, replica_groups=mesh['row'=16,'col'=32] {'row'}, dimensions={0}, use_global_device_ids=true | all-gather | bytes 278528 | tf_op jit(solution)/shard_map/all_gather | solution.py:47
  29.9 0.0 copy-done
  29.9 0.0 copy-start.3
  29.9 0.6 fusion
  30.5 0.0 copy-start.2
  30.5 27.6 %all_to_all.10 = f32[32,32,128]{2,1,0:T(8,128)} all-to-all(f32[32,32,128]{2,1,0:T(8,128)S(1)} %bitcast.4), channel_id=1, replica_groups=mesh['row'=16,'col'=32] {'col'}, dimensions={0} | all-to-all | bytes 1048576 | tf_op jit(solution)/shard_map/all_to_all | solution.py:50
  58.1 1.1 reduce_sum.9
  59.2 15.3 %all_to_all.11 = bf16[32,32,128]{2,1,0:T(8,128)(2,1)} all-to-all(bf16[32,32,128]{2,1,0:T(8,128)(2,1)S(1)} %broadcast_in_dim.2), channel_id=1, replica_groups=mesh['row'=16,'col'=32] {'col'}, dimensions={0} | all-to-all | bytes 524288 | tf_op jit(solution)/shard_map/all_to_all | solution.py:53
  74.6 0.0 all-gather.2.cloned.1.call-update
  74.6 0.1 slice_select_fusion.1
  74.7 6.4 %collective-permute-start = (f32[32,64]{1,0:T(8,128)S(1)}, f32[32,64]{1,0:T(8,128)S(1)}, u32[]{:S(2)}, u32[]{:S(2)}) collective-permute-start(f32[32,64]{1,0:T(8,128)S(1)} %get-tuple-element.2), channel_id=1, source_target_pairs={{0,1},{1,0},{2,33},{3,32},{4,65},{5,64},{6,97},{7,96},{8,129},{9,1... | collective-permute-start | bytes 24584 | tf_op jit(solution)/shard_map/ppermute | solution.py:42
  81.0 2.1 %collective-permute-start.1 = (f32[32,64]{1,0:T(8,128)S(1)}, f32[32,64]{1,0:T(8,128)S(1)}, u32[]{:S(2)}, u32[]{:S(2)}) collective-permute-start(f32[32,64]{1,0:T(8,128)S(1)} %get-tuple-element.3), channel_id=1, source_target_pairs={{0,0},{1,1},{2,32},{3,33},{4,64},{5,65},{6,96},{7,97},{8,128},{9,1... | collective-permute-start | bytes 24584 | tf_op jit(solution)/shard_map/ppermute | solution.py:41
  83.2 0.0 collective-permute-done
  83.2 4.4 %collective-permute-done.1 = f32[32,64]{1,0:T(8,128)S(1)} collective-permute-done((f32[32,64]{1,0:T(8,128)S(1)}, f32[32,64]{1,0:T(8,128)S(1)}, u32[]{:S(2)}, u32[]{:S(2)}) %collective-permute-start.1) | collective-permute-done | bytes 8224 | tf_op jit(solution)/shard_map/ppermute | solution.py:41
  87.6 0.6 maximum_select_fusion
  88.2 26.8 %all-gather.2.cloned.1.call-done.blocks_ref = bf16[16,1024,128]{2,1,0:T(8,128)(2,1)} async-done(((bf16[1,1024,128]{2,1,0:T(8,128)(2,1)}), bf16[16,1024,128]{2,1,0:T(8,128)(2,1)}) %all-gather.2.cloned.1.call-update) | async-done | bytes 4194320 | tf_op jit(solution)/shard_map/all_gather | solution.py:54
  115.0 0.0 copy-done.3
  115.0 0.0 copy-done.2
  115.0 0.0 copy-start.1
  115.0 2.2 %copy-done.1 = bf16[16,1024,128]{2,1,0:T(8,128)(2,1)S(1)} copy-done((bf16[16,1024,128]{2,1,0:T(8,128)(2,1)S(1)}, bf16[16,1024,128]{2,1,0:T(8,128)(2,1)}, u32[]{:S(2)}) %copy-start.1) | copy-done | bytes 4194328
  117.2 3.9 %shard_map.59 = f32[1024,384]{1,0:T(8,128)} custom-call(bf16[16,1024,128]{2,1,0:T(8,128)(2,1)S(1)} %copy-done.1, bf16[2048,384]{1,0:T(8,128)(2,1)S(1)} %copy-done.2, f32[1024,384]{1,0:T(8,128)S(1)} %copy-done.3), custom_call_target="tpu_custom_call" | custom-call | flops 1610612736 | bytes 9437184 | tf_op jit(solution)/shard_map/pallas_call | solution.py:19
  (2 shorter events, 0.0 us)
Async XLA Ops:
  7.2 22.8 %copy-start = (f32[64,128]{1,0:T(8,128)S(1)}, f32[64,128]{1,0:T(8,128)}, u32[]{:S(2)}) copy-start(f32[64,128]{1,0:T(8,128)} %param.5) | copy-start | bytes 98308
  7.2 107.8 %all-gather.2.cloned.1.call-start = ((), (), s32[]{:S(2)}) async-start(), calls=%async_computation.2 | async-start | bytes 4456448 | tf_op jit(solution)/shard_map/all_gather | solution.py:54
  29.9 85.1 %copy-start.3 = (f32[1024,384]{1,0:T(8,128)S(1)}, f32[1024,384]{1,0:T(8,128)}, u32[]{:S(2)}) copy-start(f32[1024,384]{1,0:T(8,128)} %trail_ref.1) | copy-start | bytes 4718596
  30.5 84.5 %copy-start.2 = (bf16[2048,384]{1,0:T(8,128)(2,1)S(1)}, bf16[2048,384]{1,0:T(8,128)(2,1)}, u32[]{:S(2)}) copy-start(bf16[2048,384]{1,0:T(8,128)(2,1)} %panel_ref.1) | copy-start | bytes 4718596
  74.7 8.5 %collective-permute-start = (f32[32,64]{1,0:T(8,128)S(1)}, f32[32,64]{1,0:T(8,128)S(1)}, u32[]{:S(2)}, u32[]{:S(2)}) collective-permute-start(f32[32,64]{1,0:T(8,128)S(1)} %get-tuple-element.2), channel_id=1, source_target_pairs={{0,1},{1,0},{2,33},{3,32},{4,65},{5,64},{6,97},{7,96},{8,129},{9,1... | collective-permute-start | bytes 24584 | tf_op jit(solution)/shard_map/ppermute | solution.py:42
  81.0 6.6 %collective-permute-start.1 = (f32[32,64]{1,0:T(8,128)S(1)}, f32[32,64]{1,0:T(8,128)S(1)}, u32[]{:S(2)}, u32[]{:S(2)}) collective-permute-start(f32[32,64]{1,0:T(8,128)S(1)} %get-tuple-element.3), channel_id=1, source_target_pairs={{0,0},{1,1},{2,32},{3,33},{4,64},{5,65},{6,96},{7,97},{8,128},{9,1... | collective-permute-start | bytes 24584 | tf_op jit(solution)/shard_map/ppermute | solution.py:41
  115.0 2.2 %copy-start.1 = (bf16[16,1024,128]{2,1,0:T(8,128)(2,1)S(1)}, bf16[16,1024,128]{2,1,0:T(8,128)(2,1)}, u32[]{:S(2)}) copy-start(bf16[16,1024,128]{2,1,0:T(8,128)(2,1)} %all-gather.2.cloned.1.call-done.blocks_ref) | copy-start | bytes 12582916
Sparse Core Ops, SparseCore 0:
  74.7 40.2 all-gather.1

commit v2 on v0

v2 whole, which is shorter than its diff:
```python
import functools

import jax
import jax.numpy as jnp
from jax import lax
from jax.experimental import pallas as pl
from jax.experimental.pallas import tpu as pltpu
from jax.sharding import Mesh, PartitionSpec as P

ROW = ("yf", "yn", "core")
COL = ("zf", "zn", "x")
FAR = ("yf", "zf")
NEAR = ("yn", "zn", "x")
SWAP = [(0, 1), (1, 0)]
TOP = 15.0


def vmem(mib):
    return pltpu.CompilerParams(vmem_limit_bytes=mib * 1024 * 1024)


def crossed(top, bottom):
    half = top.shape[1] // 2
    first = lax.broadcasted_iota(jnp.int32, top.shape, 1) < half
    return (
        jnp.where(first, top, pltpu.roll(bottom, half, 1)),
        jnp.where(first, pltpu.roll(top, half, 1), bottom),
    )


def partial_kernel(rhs_ref, band_ref, out_ref):
    band = jnp.concatenate([band_ref[i] for i in range(band_ref.shape[0])], axis=1)
    partial = jnp.dot(
        rhs_ref[...], band, preferred_element_type=jnp.float32, precision=lax.Precision.HIGHEST
    )
    largest = jnp.maximum(jnp.max(jnp.abs(partial), axis=(0, 1), keepdims=True), 2.0**-100)
    power = jnp.ceil(jnp.log2(largest))
    partial = partial * jnp.exp2(TOP - power)
    height = partial.shape[0] // 2
    for j in range(partial.shape[1] // 128):
        both = partial[:, 128 * j : 128 * (j + 1)]
        out_ref[2 * j, :height], out_ref[2 * j + 1, :height] = crossed(both[:height], both[height:])
    out_ref[:, height:] = jnp.broadcast_to(power[None], (out_ref.shape[0], 8, 128))


def partial_blocks(rhs, band):
    count, _, width = band.shape
    blocks = count * width // 64
    return pl.pallas_call(
        partial_kernel,
        out_shape=jax.ShapeDtypeStruct((blocks, rhs.shape[0] // 2 + 8, 128), jnp.float32),
        compiler_params=vmem(8),
    )(rhs, band)


def sum_kernel(shares_ref, solved_ref, low_ref):
    height, half = shares_ref.shape[1] - 8, shares_ref.shape[2] // 2
    scale = jnp.exp2(shares_ref[:, height:] - TOP)
    total = jnp.concatenate(
        [jnp.sum(shares_ref[:, i : i + 8] * scale, axis=0) for i in range(0, height, 8)], axis=0
    )
    solved_ref[:height] = total[:, :half]
    solved_ref[height:] = pltpu.roll(total, half, 1)[:, :half]
    low_ref[...] = jnp.broadcast_to(total.astype(jnp.bfloat16)[None], low_ref.shape)


def summed(shares, copies):
    height, width = shares.shape[1] - 8, shares.shape[2]
    return pl.pallas_call(
        sum_kernel,
        out_shape=(
            jax.ShapeDtypeStruct((2 * height, width // 2), jnp.float32),
            jax.ShapeDtypeStruct((copies, height, width), jnp.bfloat16),
        ),
        compiler_params=vmem(8),
    )(shares)


def stripes_kernel(core_ref, tiles_ref, panel_ref, trail_ref, *rest):
    yn = pl.program_id(0) if tiles_ref.shape[0] > 1 else 0
    _, near, far_y, far_z, _, _ = tiles_ref.shape
    rows = []
    for y in range(far_y):
        pairs = [
            crossed(tiles_ref[yn, i, y, z], tiles_ref[yn, i + 1, y, z])
            for z in range(far_z)
            for i in range(0, near, 2)
        ]
        rows += [jnp.concatenate([p[h] for p in pairs], axis=1) for h in range(2)]
    update = jnp.dot(jnp.concatenate(rows, axis=0), panel_ref[...], preferred_element_type=jnp.float32)
    out_ref = rest[-1]
    out_ref[...] = trail_ref[...] - update.reshape(out_ref.shape)


def updated_stripes(tiles, panel, trail, core, done=None):
    near_y, near, far_y, far_z, height, width = tiles.shape
    columns = panel.shape[1]
    stripe = pl.BlockSpec((far_y, 1, 1, 2 * height, columns), lambda i, core: (0, i, core[0], 0, 0))
    whole = pl.BlockSpec(memory_space=pltpu.VMEM)
    one = pl.BlockSpec((1,) + tiles.shape[1:], lambda i, core: (i, 0, 0, 0, 0, 0))
    flops = 2 * near_y * far_y * 2 * height * panel.shape[0] * columns
    return pl.pallas_call(
        stripes_kernel,
        out_shape=jax.ShapeDtypeStruct(trail.shape, jnp.float32),
        grid_spec=pltpu.PrefetchScalarGridSpec(
            num_scalar_prefetch=1,
            grid=(near_y,),
            in_specs=[whole, whole, stripe] if done is None else [one, whole, stripe, pl.BlockSpec(memory_space=pl.ANY)],
            out_specs=stripe,
        ),
        input_output_aliases={} if done is None else {4: 0},
        compiler_params=vmem(20),
        cost_estimate=pl.CostEstimate(flops=flops, bytes_accessed=5 * 1024 * 1024, transcendentals=0),
    )(core, tiles, panel, trail, *([] if done is None else [done]))


def local(size, rhs_block, diag_inverse, panel, rhs_trail):
    band = lax.all_gather(diag_inverse, ROW, axis=0, tiled=False)
    blocks = partial_blocks(rhs_block, band).astype(jnp.float16)
    shares = lax.all_to_all(blocks, COL, 0, 0, tiled=True)
    solved, low = summed(shares.astype(jnp.float32), size["yf"] * size["zf"])
    far = lax.all_to_all(low, FAR, 0, 0, tiled=True)
    copies = size["yn"] * size["zn"] * size["x"]
    near = lax.all_to_all(jnp.broadcast_to(far[None], (copies,) + far.shape), NEAR, 0, 0, tiled=True)
    tiles = near.reshape(size["yn"], size["zn"] * size["x"], size["yf"], size["zf"], *far.shape[1:])
    other = lax.ppermute(tiles, "core", SWAP)
    core = lax.axis_index("core").reshape(1)
    trail = rhs_trail.reshape(size["yf"], size["yn"], 2, 2 * far.shape[1], rhs_trail.shape[1])
    done = updated_stripes(tiles, panel, trail, core)
    done = updated_stripes(other, panel, trail, 1 - core, done)
    return solved, done.reshape(rhs_trail.shape)


def solution(mesh):
    split = Mesh(mesh.devices.reshape(4, 2, 2, 4, 2, 4), ROW + COL)
    return jax.shard_map(
        functools.partial(local, dict(split.shape)),
        mesh=split,
        in_specs=(P(ROW, COL), P(COL, ROW), P(None, ROW + COL), P(None, ROW + COL)),
        out_specs=(P(ROW, COL), P(None, ROW + COL)),
        check_vma=False,
    )
```

time: 360 us -> 110 us (0.31)
  waiting for transfers between devices: 274 us -> 0.01 us
  blocking collectives: 59.3 us -> 91.4 us
  between operations: 14.1 us -> 0.69 us
  matrix products: 9.68 us -> 0 us
  Pallas kernels: 0 us -> 7.75 us
  starting transfers between devices: 0.08 us -> 6.24 us
    unnamed x3 -> x0, waiting for transfers between devices: 215 us -> none
    all_to_all x0 -> x3, blocking collectives: none -> 68.7 us  [the longest x1 27.6 us: local(): lax.all_to_all(jnp.broadcast_to(far[None], (copies,) + far.shape), NEAR,...]
    all_gather x1 -> x0, waiting for transfers between devices: 59.8 us -> none  [local(): lax.all_gather(band, 'row', axis=0, tiled=True)]
    all_gather x2 -> x1, blocking collectives: 59.3 us -> 22.7 us  [local(): band = lax.all_gather(diag_inverse, ROW, axis=0, tiled=False)]
    pallas_call x0 -> x4, Pallas kernels: none -> 7.75 us  [the longest x2 6.06 us: updated_stripes(): pl.pallas_call(stripes_kernel, out_shape=jax.ShapeDtypeStruct(trail.shape...]
    ppermute x0 -> x1, starting transfers between devices: none -> 6.24 us  [local(): other = lax.ppermute(tiles, 'core', SWAP)]
    dot_general x1 -> x0, matrix products: 6.14 us -> none  [local(): jnp.dot(lax.all_gather(band, 'row', axis=0, tiled=True), panel, preferred...]
  transfers between devices with their start and end apart: 2 -> 1, of which waited for: 2 -> 0; matrix products, arithmetic and copies ran while one was open for 0% -> 0% of each run, Pallas kernels for 0% -> 2%
where the time goes in v2:
time: 110 us
  blocking collectives  91.4 us (83%)
  Pallas kernels  7.75 us (7%)
  starting transfers between devices  6.24 us (6%)
  local copies, waits for them, and re-layouts  3.97 us (4%)
    all_to_all x1, blocking collectives, local(): lax.all_to_all(jnp.broadcast_to(far[None], (copies,) + far.shape), NEAR,...  27.6 us
    all_to_all x1, blocking collectives, local(): shares = lax.all_to_all(blocks, COL, 0, 0, tiled=True)  23.6 us
    all_gather x1, blocking collectives, local(): band = lax.all_gather(diag_inverse, ROW, axis=0, tiled=False)  22.7 us
    all_to_all x1, blocking collectives, local(): far = lax.all_to_all(low, FAR, 0, 0, tiled=True)  17.5 us
    ppermute x1, starting transfers between devices, local(): other = lax.ppermute(tiles, 'core', SWAP)  6.24 us
    pallas_call x2, Pallas kernels, updated_stripes(): pl.pallas_call(stripes_kernel, out_shape=jax.ShapeDtypeStruct(trail.shape...  6.06 us
    unnamed x10, local copies, waits for them, and re-layouts  3.58 us
  transfers between devices with their start and end apart: 1, of which 0 were waited for; matrix products, arithmetic and copies ran while one was open for 0% of the time, Pallas kernels for 2%

profile of v2, /device:TPU:1, one launch (start us, length us, event | category | flops | bytes accessed | tf_op | source)
XLA Modules:
  0.0 110.1 jit_solution(7954205165430013494)
XLA Ops:
  0.6 22.7 %all-gather = f32[1024,128]{1,0:T(8,128)S(1)} all-gather(f32[64,128]{1,0:T(8,128)} %param.5), channel_id=2, replica_groups=mesh['yf'=4,'yn'=2,'core'=2,'zf'=4,'zn'=2,'x'=4] {'yf','yn','core'}, dimensions={0}, use_global_device_ids=true | all-gather | bytes 557056 | tf_op jit(solution)/shard_map/all_gather | solution.py:118
  23.3 0.0 copy-start.4
  23.3 0.8 copy-done.4
  24.1 0.9 shard_map.59
  25.1 23.6 %all_to_all.15 = f16[32,40,128]{2,1,0:T(8,128)(2,1)S(1)} all-to-all(f16[32,40,128]{2,1,0:T(8,128)(2,1)S(1)} %convert_element_type.6), channel_id=1, replica_groups=mesh['yf'=4,'yn'=2,'core'=2,'zf'=4,'zn'=2,'x'=4] {'zf','zn','x'}, dimensions={0} | all-to-all | bytes 655360 | tf_op jit(solution)/shard_map/all_to_all | solution.py:120
  48.7 0.8 shard_map.60
  49.4 17.5 %all_to_all.16 = bf16[16,32,128]{2,1,0:T(8,128)(2,1)S(1)} all-to-all(bf16[16,32,128]{2,1,0:T(8,128)(2,1)S(1)} %get-tuple-element.5), channel_id=1, replica_groups=mesh['yf'=4,'yn'=2,'core'=2,'zf'=4,'zn'=2,'x'=4] {'yf','zf'}, dimensions={0} | all-to-all | bytes 262144 | tf_op jit(solution)/shard_map/all_to_all | solution.py:122
  67.0 0.4 broadcast_in_dim.2
  67.4 27.6 %all_to_all.17 = bf16[16,16,32,128]{3,2,1,0:T(8,128)(2,1)S(1)} all-to-all(bf16[16,16,32,128]{3,2,1,0:T(8,128)(2,1)S(1)} %broadcast_in_dim.2), channel_id=1, replica_groups=mesh['yf'=4,'yn'=2,'core'=2,'zf'=4,'zn'=2,'x'=4] {'yn','zn','x'}, dimensions={0} | all-to-all | bytes 4194304 | tf_op jit(solution)/shard_map/all_to_all | solution.py:124
  95.0 6.2 %collective-permute-start = (bf16[2,8,4,4,32,128]{5,4,3,2,1,0:T(8,128)(2,1)S(1)}, bf16[2,8,4,4,32,128]{5,4,3,2,1,0:T(8,128)(2,1)}, u32[]{:S(2)}, u32[]{:S(2)}) collective-permute-start(bf16[2,8,4,4,32,128]{5,4,3,2,1,0:T(8,128)(2,1)S(1)} %bitcast.5), channel_id=1, source_target_pairs={{0,32},{32,0},{1,33},{33,1},{2,34},{34,2},{3,35},{35,3},{4,36},{36... | collective-permute-start | bytes 6291464 | tf_op jit(solution)/shard_map/ppermute | solution.py:126
  101.2 0.0 copy-start
  101.2 1.4 %copy-done = bf16[2048,384]{1,0:T(8,128)(2,1)S(1)} copy-done((bf16[2048,384]{1,0:T(8,128)(2,1)S(1)}, bf16[2048,384]{1,0:T(8,128)(2,1)}, u32[]{:S(2)}) %copy-start) | copy-done | bytes 1572888
  102.6 0.0 copy-start.2
  102.6 1.4 %copy-done.2 = f32[1024,384]{1,0:T(8,128)S(1)} copy-done((f32[1024,384]{1,0:T(8,128)S(1)}, f32[1024,384]{1,0:T(8,128)}, u32[]{:S(2)}) %copy-start.2) | copy-done | bytes 1572888
  104.0 0.0 copy-start.1
  104.0 0.0 copy-start.3
  104.0 2.5 %shard_map.61.rest_0_ = f32[4,2,2,64,384]{4,3,2,1,0:T(8,128)} custom-call(s32[1]{0:T(128)} %bitcast.1.core_ref, bf16[2,8,4,4,32,128]{5,4,3,2,1,0:T(8,128)(2,1)S(1)} %bitcast.6, bf16[2048,384]{1,0:T(8,128)(2,1)S(1)} %copy-done, f32[4,2,2,64,384]{4,3,2,1,0:T(8,128)S(1)} %bitcast.7), custom_call_target="tpu_custom_call" | custom-call | flops 805306368 | bytes 5242880 | tf_op jit(solution)/shard_map/pallas_call | solution.py:102
  106.5 0.0 collective-permute-done.tiles_ref
  106.5 0.0 copy-done.1
  106.5 0.0 copy-done.3
  106.5 3.6 %shard_map.62 = f32[4,2,2,64,384]{4,3,2,1,0:T(8,128)} custom-call(s32[1]{0:T(128)S(6)} %sub.3.core_ref, bf16[2,8,4,4,32,128]{5,4,3,2,1,0:T(8,128)(2,1)} %collective-permute-done.tiles_ref, bf16[2048,384]{1,0:T(8,128)(2,1)S(1)} %copy-done.1, f32[4,2,2,64,384]{4,3,2,1,0:T(8,128)S(1)} %bitcast.8, ...), custom_call_target="tpu_custom_call", output_to_operand_aliasing={{}: (4, {})} | custom-call | flops 805306368 | bytes 5242880 | tf_op jit(solution)/shard_map/pallas_call | solution.py:102
  (2 shorter events, 0.1 us)
Async XLA Ops:
  23.3 0.8 copy-start.4
  95.0 11.6 %collective-permute-start = (bf16[2,8,4,4,32,128]{5,4,3,2,1,0:T(8,128)(2,1)S(1)}, bf16[2,8,4,4,32,128]{5,4,3,2,1,0:T(8,128)(2,1)}, u32[]{:S(2)}, u32[]{:S(2)}) collective-permute-start(bf16[2,8,4,4,32,128]{5,4,3,2,1,0:T(8,128)(2,1)S(1)} %bitcast.5), channel_id=1, source_target_pairs={{0,32},{32,0},{1,33},{33,1},{2,34},{34,2},{3,35},{35,3},{4,36},{36... | collective-permute-start | bytes 6291464 | tf_op jit(solution)/shard_map/ppermute | solution.py:126
  101.2 1.4 %copy-start = (bf16[2048,384]{1,0:T(8,128)(2,1)S(1)}, bf16[2048,384]{1,0:T(8,128)(2,1)}, u32[]{:S(2)}) copy-start(bf16[2048,384]{1,0:T(8,128)(2,1)} %panel_ref.3) | copy-start | bytes 4718596
  102.6 1.4 %copy-start.2 = (f32[1024,384]{1,0:T(8,128)S(1)}, f32[1024,384]{1,0:T(8,128)}, u32[]{:S(2)}) copy-start(f32[1024,384]{1,0:T(8,128)} %param.7) | copy-start | bytes 4718596
  104.0 2.5 %copy-start.1 = (bf16[2048,384]{1,0:T(8,128)(2,1)S(1)}, bf16[2048,384]{1,0:T(8,128)(2,1)}, u32[]{:S(2)}) copy-start(bf16[2048,384]{1,0:T(8,128)(2,1)} %panel_ref.3) | copy-start | bytes 4718596
  104.0 2.5 %copy-start.3 = (f32[1024,384]{1,0:T(8,128)S(1)}, f32[1024,384]{1,0:T(8,128)}, u32[]{:S(2)}) copy-start(f32[1024,384]{1,0:T(8,128)} %param.7) | copy-start | bytes 4718596

commit v3 on v2

--- a/solution.py
+++ b/solution.py
@@ -8,9 +8,9 @@
 from jax.sharding import Mesh, PartitionSpec as P
 
 ROW = ("yf", "yn", "core")
-COL = ("zf", "zn", "x")
-FAR = ("yf", "zf")
-NEAR = ("yn", "zn", "x")
+COL = ("zf", "zn", "xf", "xn")
+FAR = ("yf", "zf", "xf")
+NEAR = ("yn", "zn", "xn")
 SWAP = [(0, 1), (1, 0)]
 TOP = 15.0
 
@@ -78,13 +78,14 @@
 
 def stripes_kernel(core_ref, tiles_ref, panel_ref, trail_ref, *rest):
     yn = pl.program_id(0) if tiles_ref.shape[0] > 1 else 0
-    _, near, far_y, far_z, _, _ = tiles_ref.shape
+    _, near_z, _, far_y, far_z, far_x, _, _ = tiles_ref.shape
     rows = []
     for y in range(far_y):
         pairs = [
-            crossed(tiles_ref[yn, i, y, z], tiles_ref[yn, i + 1, y, z])
+            crossed(tiles_ref[yn, n, 0, y, z, x], tiles_ref[yn, n, 1, y, z, x])
             for z in range(far_z)
-            for i in range(0, near, 2)
+            for n in range(near_z)
+            for x in range(far_x)
         ]
         rows += [jnp.concatenate([p[h] for p in pairs], axis=1) for h in range(2)]
     update = jnp.dot(jnp.concatenate(rows, axis=0), panel_ref[...], preferred_element_type=jnp.float32)
@@ -93,11 +94,11 @@
 
 
 def updated_stripes(tiles, panel, trail, core, done=None):
-    near_y, near, far_y, far_z, height, width = tiles.shape
+    near_y, far_y, height = tiles.shape[0], tiles.shape[3], tiles.shape[6]
     columns = panel.shape[1]
     stripe = pl.BlockSpec((far_y, 1, 1, 2 * height, columns), lambda i, core: (0, i, core[0], 0, 0))
     whole = pl.BlockSpec(memory_space=pltpu.VMEM)
-    one = pl.BlockSpec((1,) + tiles.shape[1:], lambda i, core: (i, 0, 0, 0, 0, 0))
+    one = pl.BlockSpec((1,) + tiles.shape[1:], lambda i, core: (i,) + (0,) * 7)
     flops = 2 * near_y * far_y * 2 * height * panel.shape[0] * columns
     return pl.pallas_call(
         stripes_kernel,
@@ -114,15 +115,40 @@
     )(core, tiles, panel, trail, *([] if done is None else [done]))
 
 
+def cubes(size):
+    count_y, count_z, count_x = 2 * size["yf"], 2 * size["zf"], 2 * size["xf"]
+
+    def device(y, core, z, x):
+        return ((y % count_y * size["core"] + core) * count_z + z % count_z) * count_x + x % count_x
+
+    def place(corner, parity, core):
+        return corner + (2 - parity if core else parity)
+
+    return [
+        [
+            device(place(y, a, core), core, place(z, b, core), place(x, c, core))
+            for a in range(2)
+            for b in range(2)
+            for c in range(2)
+        ]
+        for y in range(0, count_y, 2)
+        for core in range(size["core"])
+        for z in range(0, count_z, 2)
+        for x in range(0, count_x, 2)
+    ]
+
+
 def local(size, rhs_block, diag_inverse, panel, rhs_trail):
     band = lax.all_gather(diag_inverse, ROW, axis=0, tiled=False)
     blocks = partial_blocks(rhs_block, band).astype(jnp.float16)
     shares = lax.all_to_all(blocks, COL, 0, 0, tiled=True)
-    solved, low = summed(shares.astype(jnp.float32), size["yf"] * size["zf"])
+    solved, low = summed(shares.astype(jnp.float32), size["yf"] * size["zf"] * size["xf"])
     far = lax.all_to_all(low, FAR, 0, 0, tiled=True)
-    copies = size["yn"] * size["zn"] * size["x"]
-    near = lax.all_to_all(jnp.broadcast_to(far[None], (copies,) + far.shape), NEAR, 0, 0, tiled=True)
-    tiles = near.reshape(size["yn"], size["zn"] * size["x"], size["yf"], size["zf"], *far.shape[1:])
+    copies = size["yn"] * size["zn"] * size["xn"]
+    near = lax.all_to_all(
+        jnp.broadcast_to(far[None], (copies,) + far.shape), ROW + COL, 0, 0, tiled=True, axis_index_groups=cubes(size)
+    )
+    tiles = near.reshape(tuple(size[a] for a in NEAR + FAR) + far.shape[1:])
     other = lax.ppermute(tiles, "core", SWAP)
     core = lax.axis_index("core").reshape(1)
     trail = rhs_trail.reshape(size["yf"], size["yn"], 2, 2 * far.shape[1], rhs_trail.shape[1])
@@ -132,7 +158,7 @@
 
 
 def solution(mesh):
-    split = Mesh(mesh.devices.reshape(4, 2, 2, 4, 2, 4), ROW + COL)
+    split = Mesh(mesh.devices.reshape(4, 2, 2, 4, 2, 2, 2), ROW + COL)
     return jax.shard_map(
         functools.partial(local, dict(split.shape)),
         mesh=split,

time: 110 us -> 105 us (0.955)
  starting transfers between devices: 6.24 us -> 1.91 us
    ppermute x1, starting transfers between devices: 6.24 us -> 1.91 us  [local(): other = lax.ppermute(tiles, 'core', SWAP)]
    all_to_all x1, blocking collectives: 27.6 us -> 23.7 us  [local(): lax.all_to_all(jnp.broadcast_to(far[None], (copies,) + far.shape), ROW +...]
    all_to_all x1, blocking collectives: 17.5 us -> 20.7 us  [local(): far = lax.all_to_all(low, FAR, 0, 0, tiled=True)]
where the time goes in v3:
time: 105 us
  blocking collectives  90.7 us (86%)
  Pallas kernels  7.69 us (7%)
  local copies, waits for them, and re-layouts  3.93 us (4%)
  starting transfers between devices  1.91 us (2%)
    all_to_all x1, blocking collectives, local(): lax.all_to_all(jnp.broadcast_to(far[None], (copies,) + far.shape), ROW +...  23.7 us
    all_to_all x1, blocking collectives, local(): shares = lax.all_to_all(blocks, COL, 0, 0, tiled=True)  23.6 us
    all_gather x1, blocking collectives, local(): band = lax.all_gather(diag_inverse, ROW, axis=0, tiled=False)  22.7 us
    all_to_all x1, blocking collectives, local(): far = lax.all_to_all(low, FAR, 0, 0, tiled=True)  20.7 us
    pallas_call x2, Pallas kernels, updated_stripes(): pl.pallas_call(stripes_kernel, out_shape=jax.ShapeDtypeStruct(trail.shape...  6.01 us
    unnamed x10, local copies, waits for them, and re-layouts  3.58 us
  transfers between devices with their start and end apart: 1, of which 0 were waited for; matrix products, arithmetic and copies ran while one was open for 0% of the time, Pallas kernels for 2%

profile of v3, /device:TPU:1, one launch (start us, length us, event | category | flops | bytes accessed | tf_op | source)
XLA Modules:
  0.0 105.0 jit_solution(10316794579391693805)
XLA Ops:
  0.6 22.7 %all-gather = f32[1024,128]{1,0:T(8,128)S(1)} all-gather(f32[64,128]{1,0:T(8,128)} %param.5), channel_id=2, replica_groups=mesh['yf'=4,'yn'=2,'core'=2,'zf'=4,'zn'=2,'xf'=2,'xn'=2] {'yf','yn','core'}, dimensions={0}, use_global_device_ids=true | all-gather | bytes 557056 | tf_op jit(solution)/shard_map/all_gather | solution.py:142
  23.3 0.0 copy-start.4
  23.3 0.8 copy-done.4
  24.1 0.9 shard_map.59
  25.1 23.6 %all_to_all.15 = f16[32,40,128]{2,1,0:T(8,128)(2,1)S(1)} all-to-all(f16[32,40,128]{2,1,0:T(8,128)(2,1)S(1)} %convert_element_type.6), channel_id=1, replica_groups=mesh['yf'=4,'yn'=2,'core'=2,'zf'=4,'zn'=2,'xf'=2,'xn'=2] {'zf','zn','xf'..., dimensions={0} | all-to-all | bytes 655360 | tf_op jit(solution)/shard_map/all_to_all | solution.py:144
  48.7 0.8 shard_map.60
  49.4 20.7 %all_to_all.16 = bf16[32,32,128]{2,1,0:T(8,128)(2,1)S(1)} all-to-all(bf16[32,32,128]{2,1,0:T(8,128)(2,1)S(1)} %get-tuple-element.5), channel_id=1, replica_groups=mesh['yf'=4,'yn'=2,'core'=2,'zf'=4,'zn'=2,'xf'=2,'xn'=2] {'yf','zf','xf'}, dimensions={0} | all-to-all | bytes 524288 | tf_op jit(solution)/shard_map/all_to_all | solution.py:146
  70.1 0.3 broadcast_in_dim.2
  70.5 23.7 %all_to_all.17 = bf16[8,32,32,128]{3,2,1,0:T(8,128)(2,1)S(1)} all-to-all(bf16[8,32,32,128]{3,2,1,0:T(8,128)(2,1)S(1)} %broadcast_in_dim.2), channel_id=1, replica_groups={{0,1,4,5,64,65,68,69},{2,3,6,7,66,67,70,71},{8,9,12,13,72,73,76,77},{10..., dimensions={0} | all-to-all | bytes 4194304 | tf_op jit(solution)/shard_map/all_to_all | solution.py:148
  94.2 1.9 %collective-permute-start = (bf16[2,2,2,4,4,2,32,128]{7,6,5,4,3,2,1,0:T(8,128)(2,1)S(1)}, bf16[2,2,2,4,4,2,32,128]{7,6,5,4,3,2,1,0:T(8,128)(2,1)}, u32[]{:S(2)}, u32[]{:S(2)}) collective-permute-start(bf16[2,2,2,4,4,2,32,128]{7,6,5,4,3,2,1,0:T(8,128)(2,1)S(1)} %bitcast.5), channel_id=1, source_target_pairs={{0,32},{32,0},{1,33},{33,1},{2,34},{34,2},{3,35},{35,3},{4,36},{36... | collective-permute-start | bytes 6291464 | tf_op jit(solution)/shard_map/ppermute | solution.py:152
  96.1 0.0 copy-start
  96.1 1.4 %copy-done = bf16[2048,384]{1,0:T(8,128)(2,1)S(1)} copy-done((bf16[2048,384]{1,0:T(8,128)(2,1)S(1)}, bf16[2048,384]{1,0:T(8,128)(2,1)}, u32[]{:S(2)}) %copy-start) | copy-done | bytes 1572888
  97.5 0.0 copy-start.2
  97.5 1.4 %copy-done.2 = f32[1024,384]{1,0:T(8,128)S(1)} copy-done((f32[1024,384]{1,0:T(8,128)S(1)}, f32[1024,384]{1,0:T(8,128)}, u32[]{:S(2)}) %copy-start.2) | copy-done | bytes 1572888
  98.9 0.0 copy-start.1
  98.9 0.0 copy-start.3
  98.9 2.4 %shard_map.61.rest_0_ = f32[4,2,2,64,384]{4,3,2,1,0:T(8,128)} custom-call(s32[1]{0:T(128)} %bitcast.1.core_ref, bf16[2,2,2,4,4,2,32,128]{7,6,5,4,3,2,1,0:T(8,128)(2,1)S(1)} %bitcast.6, bf16[2048,384]{1,0:T(8,128)(2,1)S(1)} %copy-done, f32[4,2,2,64,384]{4,3,2,1,0:T(8,128)S(1)} %bitcast.7), custom_call_target="tpu_custom_call" | custom-call | flops 805306368 | bytes 5242880 | tf_op jit(solution)/shard_map/pallas_call | solution.py:103
  101.4 0.0 collective-permute-done.tiles_ref
  101.4 0.0 copy-done.1
  101.4 0.0 copy-done.3
  101.4 3.6 %shard_map.62 = f32[4,2,2,64,384]{4,3,2,1,0:T(8,128)} custom-call(s32[1]{0:T(128)S(6)} %sub.3.core_ref, bf16[2,2,2,4,4,2,32,128]{7,6,5,4,3,2,1,0:T(8,128)(2,1)} %collective-permute-done.tiles_ref, bf16[2048,384]{1,0:T(8,128)(2,1)S(1)} %copy-done.1, f32[4,2,2,64,384]{4,3,2,1,0:T(8,128)S(1)} %bitcast.8, ...), custom_call_target="tpu_custom_call", output_to_operand_aliasing={{}: (4, {})} | custom-call | flops 805306368 | bytes 5242880 | tf_op jit(solution)/shard_map/pallas_call | solution.py:103
  (2 shorter events, 0.1 us)
Async XLA Ops:
  23.3 0.8 copy-start.4
  94.2 7.2 %collective-permute-start = (bf16[2,2,2,4,4,2,32,128]{7,6,5,4,3,2,1,0:T(8,128)(2,1)S(1)}, bf16[2,2,2,4,4,2,32,128]{7,6,5,4,3,2,1,0:T(8,128)(2,1)}, u32[]{:S(2)}, u32[]{:S(2)}) collective-permute-start(bf16[2,2,2,4,4,2,32,128]{7,6,5,4,3,2,1,0:T(8,128)(2,1)S(1)} %bitcast.5), channel_id=1, source_target_pairs={{0,32},{32,0},{1,33},{33,1},{2,34},{34,2},{3,35},{35,3},{4,36},{36... | collective-permute-start | bytes 6291464 | tf_op jit(solution)/shard_map/ppermute | solution.py:152
  96.1 1.4 %copy-start = (bf16[2048,384]{1,0:T(8,128)(2,1)S(1)}, bf16[2048,384]{1,0:T(8,128)(2,1)}, u32[]{:S(2)}) copy-start(bf16[2048,384]{1,0:T(8,128)(2,1)} %panel_ref.3) | copy-start | bytes 4718596
  97.5 1.4 %copy-start.2 = (f32[1024,384]{1,0:T(8,128)S(1)}, f32[1024,384]{1,0:T(8,128)}, u32[]{:S(2)}) copy-start(f32[1024,384]{1,0:T(8,128)} %param.7) | copy-start | bytes 4718596
  98.9 2.4 %copy-start.1 = (bf16[2048,384]{1,0:T(8,128)(2,1)S(1)}, bf16[2048,384]{1,0:T(8,128)(2,1)}, u32[]{:S(2)}) copy-start(bf16[2048,384]{1,0:T(8,128)(2,1)} %panel_ref.3) | copy-start | bytes 4718596
  98.9 2.4 %copy-start.3 = (f32[1024,384]{1,0:T(8,128)S(1)}, f32[1024,384]{1,0:T(8,128)}, u32[]{:S(2)}) copy-start(f32[1024,384]{1,0:T(8,128)} %param.7) | copy-start | bytes 4718596

commit v4 on v3

--- a/solution.py
+++ b/solution.py
@@ -9,8 +9,8 @@
 
 ROW = ("yf", "yn", "core")
 COL = ("zf", "zn", "xf", "xn")
-FAR = ("yf", "zf", "xf")
-NEAR = ("yn", "zn", "xn")
+FAR = ("zf", "yf", "xf")
+NEAR = ("zn", "yn", "xn")
 SWAP = [(0, 1), (1, 0)]
 TOP = 15.0
 
@@ -28,32 +28,42 @@
     )
 
 
-def partial_kernel(rhs_ref, band_ref, out_ref):
-    band = jnp.concatenate([band_ref[i] for i in range(band_ref.shape[0])], axis=1)
+def partial_kernel(rhs_ref, mine_ref, other_ref, core_ref, out_ref):
+    count, height, half = rhs_ref.shape[0], rhs_ref.shape[1], rhs_ref.shape[2] // 2
+    rows = []
+    for i in range(count):
+        both = rhs_ref[i]
+        rows += [both[:, :half], pltpu.roll(both, half, 1)[:, :half]]
+    first = core_ref[0] == 0
+    mine, other = mine_ref[...], other_ref[...]
+    inverse = jnp.concatenate([jnp.where(first, mine, other), jnp.where(first, other, mine)], axis=1)
     partial = jnp.dot(
-        rhs_ref[...], band, preferred_element_type=jnp.float32, precision=lax.Precision.HIGHEST
+        jnp.concatenate(rows, axis=0), inverse, preferred_element_type=jnp.float32, precision=lax.Precision.HIGHEST
     )
     largest = jnp.maximum(jnp.max(jnp.abs(partial), axis=(0, 1), keepdims=True), 2.0**-100)
     power = jnp.ceil(jnp.log2(largest))
     partial = partial * jnp.exp2(TOP - power)
-    height = partial.shape[0] // 2
-    for j in range(partial.shape[1] // 128):
-        both = partial[:, 128 * j : 128 * (j + 1)]
-        out_ref[2 * j, :height], out_ref[2 * j + 1, :height] = crossed(both[:height], both[height:])
+    block = 0
+    for i in range(count):
+        for j in range(partial.shape[1] // 128):
+            both = partial[2 * height * i : 2 * height * (i + 1), 128 * j : 128 * (j + 1)]
+            out_ref[block, :height], out_ref[block + 1, :height] = crossed(both[:height], both[height:])
+            block += 2
     out_ref[:, height:] = jnp.broadcast_to(power[None], (out_ref.shape[0], 8, 128))
 
 
-def partial_blocks(rhs, band):
-    count, _, width = band.shape
-    blocks = count * width // 64
+def partial_blocks(rhs, mine, other, core):
+    count, height, _ = rhs.shape
+    whole = pl.BlockSpec(memory_space=pltpu.VMEM)
     return pl.pallas_call(
         partial_kernel,
-        out_shape=jax.ShapeDtypeStruct((blocks, rhs.shape[0] // 2 + 8, 128), jnp.float32),
+        out_shape=jax.ShapeDtypeStruct((count * 2 * mine.shape[1] // 64, height + 8, 128), jnp.float32),
+        in_specs=[whole, whole, whole, pl.BlockSpec(memory_space=pltpu.SMEM)],
         compiler_params=vmem(8),
-    )(rhs, band)
+    )(rhs, mine, other, core)
 
 
-def sum_kernel(shares_ref, solved_ref, low_ref):
+def sum_kernel(shares_ref, panel_ref, trail_ref, solved_ref, low_ref):
     height, half = shares_ref.shape[1] - 8, shares_ref.shape[2] // 2
     scale = jnp.exp2(shares_ref[:, height:] - TOP)
     total = jnp.concatenate(
@@ -64,7 +74,7 @@
     low_ref[...] = jnp.broadcast_to(total.astype(jnp.bfloat16)[None], low_ref.shape)
 
 
-def summed(shares, copies):
+def summed(shares, copies, panel, trail):
     height, width = shares.shape[1] - 8, shares.shape[2]
     return pl.pallas_call(
         sum_kernel,
@@ -73,7 +83,7 @@
             jax.ShapeDtypeStruct((copies, height, width), jnp.bfloat16),
         ),
         compiler_params=vmem(8),
-    )(shares)
+    )(shares, panel, trail)
 
 
 def stripes_kernel(core_ref, tiles_ref, panel_ref, trail_ref, *rest):
@@ -126,7 +136,7 @@
 
     return [
         [
-            device(place(y, a, core), core, place(z, b, core), place(x, c, core))
+            device(place(y, b, core), core, place(z, a, core), place(x, c, core))
             for a in range(2)
             for b in range(2)
             for c in range(2)
@@ -139,19 +149,31 @@
 
 
 def local(size, rhs_block, diag_inverse, panel, rhs_trail):
-    band = lax.all_gather(diag_inverse, ROW, axis=0, tiled=False)
-    blocks = partial_blocks(rhs_block, band).astype(jnp.float16)
+    core = lax.axis_index("core").reshape(1)
+    other_inverse = lax.ppermute(diag_inverse, "core", SWAP)
+    half, count_y, count_z = rhs_block.shape[0] // 2, size["yf"] * size["yn"], size["zf"] * size["zn"]
+    rows = jnp.concatenate([rhs_block[:half], rhs_block[half:]], axis=1)
+    rows = lax.all_to_all(jnp.broadcast_to(rows[None], (count_y,) + rows.shape), ("yf", "yn"), 0, 0, tiled=True)
+    blocks = partial_blocks(rows, diag_inverse, other_inverse, core).astype(jnp.float16)
     shares = lax.all_to_all(blocks, COL, 0, 0, tiled=True)
-    solved, low = summed(shares.astype(jnp.float32), size["yf"] * size["zf"] * size["xf"])
-    far = lax.all_to_all(low, FAR, 0, 0, tiled=True)
+    trail = rhs_trail.reshape(size["zf"], size["zn"], 2, 2 * half, rhs_trail.shape[1])
+    solved, low = summed(shares.astype(jnp.float32), size["yf"] * size["zf"] * size["xf"], panel, trail)
+    count_x = size["xf"] * size["xn"]
+    swapped = [
+        (((y * 2 + k) * count_z + z) * count_x + x, ((z * 2 + k) * count_y + y) * count_x + x)
+        for y in range(count_y)
+        for k in range(2)
+        for z in range(count_z)
+        for x in range(count_x)
+    ]
+    solved = lax.ppermute(solved, ROW + COL, swapped)
+    far, solved = lax.optimization_barrier((lax.all_to_all(low, FAR, 0, 0, tiled=True), solved))
     copies = size["yn"] * size["zn"] * size["xn"]
     near = lax.all_to_all(
         jnp.broadcast_to(far[None], (copies,) + far.shape), ROW + COL, 0, 0, tiled=True, axis_index_groups=cubes(size)
     )
     tiles = near.reshape(tuple(size[a] for a in NEAR + FAR) + far.shape[1:])
     other = lax.ppermute(tiles, "core", SWAP)
-    core = lax.axis_index("core").reshape(1)
-    trail = rhs_trail.reshape(size["yf"], size["yn"], 2, 2 * far.shape[1], rhs_trail.shape[1])
     done = updated_stripes(tiles, panel, trail, core)
     done = updated_stripes(other, panel, trail, 1 - core, done)
     return solved, done.reshape(rhs_trail.shape)

time: 105 us -> 98.8 us (0.941)
  blocking collectives: 90.7 us -> 45.1 us
  starting transfers between devices: 1.91 us -> 23.3 us
  waiting for transfers between devices: 0.01 us -> 19.2 us
  Pallas kernels: 7.69 us -> 6.61 us
    all_gather x1 -> x0, blocking collectives: 22.7 us -> none  [local(): band = lax.all_gather(diag_inverse, ROW, axis=0, tiled=False)]
    all_to_all x1 -> x0, blocking collectives: 20.7 us -> none  [local(): far = lax.all_to_all(low, FAR, 0, 0, tiled=True)]
    all_to_all x0 -> x2, waiting for transfers between devices: none -> 16.8 us  [the longest x1 14.4 us: local(): lax.all_to_all(low, FAR, 0, 0, tiled=True)]
    all_to_all x0 -> x2, starting transfers between devices: none -> 15.7 us  [the longest x1 8.01 us: local(): lax.all_to_all(low, FAR, 0, 0, tiled=True)]
    ppermute x0 -> x2, starting transfers between devices: none -> 5.18 us  [the longest x1 4.52 us: local(): other_inverse = lax.ppermute(diag_inverse, 'core', SWAP)]
    unnamed x10 -> x7, local copies, waits for them, and re-layouts: 3.58 us -> 1.38 us
    all_to_all x1, blocking collectives: 23.7 us -> 21.7 us  [local(): lax.all_to_all(jnp.broadcast_to(far[None], (copies,) + far.shape), ROW +...]
    ppermute x1, waiting for transfers between devices: 0.01 us -> 1.33 us  [local(): other = lax.ppermute(tiles, 'core', SWAP)]
  transfers between devices with their start and end apart: 1 -> 5, of which waited for: 0 -> 4; matrix products, arithmetic and copies ran while one was open for 0% -> 0% of each run, Pallas kernels for 2% -> 2%
where the time goes in v4:
time: 98.8 us; the launch traced here: 98.2 us
  blocking collectives  45.1 us (46%)
  starting transfers between devices  23.3 us (24%)
  waiting for transfers between devices  19.2 us (19%)
  Pallas kernels  6.61 us (7%)
  local copies, waits for them, and re-layouts  3.14 us (3%)
    all_to_all x1, blocking collectives, local(): shares = lax.all_to_all(blocks, COL, 0, 0, tiled=True)  23.3 us
    all_to_all x1, blocking collectives, local(): lax.all_to_all(jnp.broadcast_to(far[None], (copies,) + far.shape), ROW +...  21.7 us
    all_to_all x1, waiting for transfers between devices, local(): lax.all_to_all(low, FAR, 0, 0, tiled=True)  14.4 us
    all_to_all x1, starting transfers between devices, local(): lax.all_to_all(low, FAR, 0, 0, tiled=True)  8.01 us
    all_to_all x1, starting transfers between devices, local(): lax.all_to_all(jnp.broadcast_to(rows[None], (count_y,) + rows.shape), ('y...  7.65 us
    pallas_call x2, Pallas kernels, updated_stripes(): pl.pallas_call(stripes_kernel, out_shape=jax.ShapeDtypeStruct(trail.shape...  4.87 us
    ppermute x1, starting transfers between devices, local(): other_inverse = lax.ppermute(diag_inverse, 'core', SWAP)  4.52 us
    ppermute x1, starting transfers between devices, local(): other = lax.ppermute(tiles, 'core', SWAP)  2.49 us
  transfers between devices with their start and end apart: 5, of which 4 were waited for; matrix products, arithmetic and copies ran while one was open for 0% of the time, Pallas kernels for 2%

profile of v4, /device:TPU:1, one launch (start us, length us, event | category | flops | bytes accessed | tf_op | source)
XLA Modules:
  0.0 98.2 jit_solution(7547982985927407731)
XLA Ops:
  0.6 0.7 fusion
  1.4 0.1 pad_maximum_fusion
  1.4 0.7 broadcast_in_dim.4
  2.1 7.7 %all-to-all-start = ((f32[8,32,128]{2,1,0:T(8,128)}), f32[8,32,128]{2,1,0:T(8,128)S(1)}, u32[]{:S(2)}, u32[]{:S(2)}) async-start(f32[8,32,128]{2,1,0:T(8,128)} %broadcast_in_dim.4), calls=%async_computation | async-start | bytes 262144 | tf_op jit(solution)/shard_map/all_to_all | solution.py:156
  9.8 4.5 %collective-permute-start = (f32[64,128]{1,0:T(8,128)}, f32[64,128]{1,0:T(8,128)S(1)}, u32[]{:S(2)}, u32[]{:S(2)}) collective-permute-start(f32[64,128]{1,0:T(8,128)} %mine_ref.1), channel_id=1, source_target_pairs={{0,32},{32,0},{1,33},{33,1},{2,34},{34,2},{3,35},{35,3},{4,36},{36... | collective-permute-start | bytes 98312 | tf_op jit(solution)/shard_map/ppermute | solution.py:153
  14.3 1.0 %collective-permute-done.other_ref = f32[64,128]{1,0:T(8,128)S(1)} collective-permute-done((f32[64,128]{1,0:T(8,128)}, f32[64,128]{1,0:T(8,128)S(1)}, u32[]{:S(2)}, u32[]{:S(2)}) %collective-permute-start) | collective-permute-done | bytes 32800 | tf_op jit(solution)/shard_map/ppermute | solution.py:153
  15.3 2.5 %all-to-all-done.rhs_ref = f32[8,32,128]{2,1,0:T(8,128)S(1)} async-done(((f32[8,32,128]{2,1,0:T(8,128)}), f32[8,32,128]{2,1,0:T(8,128)S(1)}, u32[]{:S(2)}, u32[]{:S(2)}) %all-to-all-start) | async-done | bytes 131104 | tf_op jit(solution)/shard_map/all_to_all | solution.py:156
  17.8 0.8 copy-done.2
  18.6 1.0 shard_map.59
  19.6 23.3 %all_to_all.20 = f16[32,40,128]{2,1,0:T(8,128)(2,1)S(1)} all-to-all(f16[32,40,128]{2,1,0:T(8,128)(2,1)S(1)} %convert_element_type.6), channel_id=1, replica_groups=mesh['yf'=4,'yn'=2,'core'=2,'zf'=4,'zn'=2,'xf'=2,'xn'=2] {'zf','zn','xf'..., dimensions={0} | all-to-all | bytes 655360 | tf_op jit(solution)/shard_map/all_to_all | solution.py:158
  42.9 0.0 copy-done
  43.0 0.0 copy-done.1
  43.0 0.8 shard_map.60
  43.7 8.0 %all-to-all-start.2 = ((bf16[32,32,128]{2,1,0:T(8,128)(2,1)}), bf16[32,32,128]{2,1,0:T(8,128)(2,1)S(1)}, u32[]{:S(2)}, u32[]{:S(2)}) async-start(bf16[32,32,128]{2,1,0:T(8,128)(2,1)} %get-tuple-element.6), calls=%async_computation.2 | async-start | bytes 524288 | tf_op jit(solution)/shard_map/all_to_all | solution.py:170
  51.8 0.7 collective-permute-start.1
  52.4 0.0 collective-permute-done.1
  52.4 14.4 %all-to-all-done.2 = bf16[32,32,128]{2,1,0:T(8,128)(2,1)S(1)} async-done(((bf16[32,32,128]{2,1,0:T(8,128)(2,1)}), bf16[32,32,128]{2,1,0:T(8,128)(2,1)S(1)}, u32[]{:S(2)}, u32[]{:S(2)}) %all-to-all-start.2) | async-done | bytes 262176 | tf_op jit(solution)/shard_map/all_to_all | solution.py:170
  66.8 0.3 broadcast_in_dim.5
  67.2 21.7 %all_to_all.21 = bf16[8,32,32,128]{3,2,1,0:T(8,128)(2,1)S(1)} all-to-all(bf16[8,32,32,128]{3,2,1,0:T(8,128)(2,1)S(1)} %broadcast_in_dim.5), channel_id=1, replica_groups={{0,1,64,65,4,5,68,69},{2,3,66,67,6,7,70,71},{8,9,72,73,12,13,76,77},{10..., dimensions={0} | all-to-all | bytes 4194304 | tf_op jit(solution)/shard_map/all_to_all | solution.py:172
  88.9 2.5 %collective-permute-start.2 = (bf16[2,2,2,4,4,2,32,128]{7,6,5,4,3,2,1,0:T(8,128)(2,1)S(1)}, bf16[2,2,2,4,4,2,32,128]{7,6,5,4,3,2,1,0:T(8,128)(2,1)S(1)}, u32[]{:S(2)}, u32[]{:S(2)}) collective-permute-start(bf16[2,2,2,4,4,2,32,128]{7,6,5,4,3,2,1,0:T(8,128)(2,1)S(1)} %bitcast.7), channel_id=1, source_target_pairs={{0,32},{32,0},{1,33},{33,1},{2,34},{34,2},{3,35},{35,3},{4,36},{36... | collective-permute-start | bytes 6291464 | tf_op jit(solution)/shard_map/ppermute | solution.py:176
  91.4 2.4 %shard_map.61.rest_0_ = f32[4,2,2,64,384]{4,3,2,1,0:T(8,128)} custom-call(s32[1]{0:T(128)} %bitcast.core_ref, bf16[2,2,2,4,4,2,32,128]{7,6,5,4,3,2,1,0:T(8,128)(2,1)S(1)} %bitcast.8, bf16[2048,384]{1,0:T(8,128)(2,1)S(1)} %copy-done, f32[4,2,2,64,384]{4,3,2,1,0:T(8,128)S(1)} %bitcast.5), custom_call_target="tpu_custom_call" | custom-call | flops 805306368 | bytes 5242880 | tf_op jit(solution)/shard_map/pallas_call | solution.py:113
  93.8 1.3 %collective-permute-done.2.tiles_ref = bf16[2,2,2,4,4,2,32,128]{7,6,5,4,3,2,1,0:T(8,128)(2,1)S(1)} collective-permute-done((bf16[2,2,2,4,4,2,32,128]{7,6,5,4,3,2,1,0:T(8,128)(2,1)S(1)}, bf16[2,2,2,4,4,2,32,128]{7,6,5,4,3,2,1,0:T(8,128)(2,1)S(1)}, u32[]{:S(2)}, u32[]{:S(2)}) %collective-permute-start.2) | collective-permute-done | bytes 2097184 | tf_op jit(solution)/shard_map/ppermute | solution.py:176
  95.2 2.4 %shard_map.62 = f32[4,2,2,64,384]{4,3,2,1,0:T(8,128)} custom-call(s32[1]{0:T(128)S(6)} %sub.3.core_ref, bf16[2,2,2,4,4,2,32,128]{7,6,5,4,3,2,1,0:T(8,128)(2,1)S(1)} %collective-permute-done.2.tiles_ref, bf16[2048,384]{1,0:T(8,128)(2,1)S(1)} %copy-done, f32[4,2,2,64,384]{4,3,2,1,0:T(8,128)S(1)} %bitcast.6, ...), custom_call_target="tpu_custom_call", output_to_operand_aliasing={{}: (4, {})} | custom-call | flops 805306368 | bytes 5242880 | tf_op jit(solution)/shard_map/pallas_call | solution.py:113
  97.6 0.6 copy.9
  (5 shorter events, 0.1 us)
Async XLA Ops:
  2.1 15.7 %all-to-all-start = ((f32[8,32,128]{2,1,0:T(8,128)}), f32[8,32,128]{2,1,0:T(8,128)S(1)}, u32[]{:S(2)}, u32[]{:S(2)}) async-start(f32[8,32,128]{2,1,0:T(8,128)} %broadcast_in_dim.4), calls=%async_computation | async-start | bytes 262144 | tf_op jit(solution)/shard_map/all_to_all | solution.py:156
  9.8 5.6 %collective-permute-start = (f32[64,128]{1,0:T(8,128)}, f32[64,128]{1,0:T(8,128)S(1)}, u32[]{:S(2)}, u32[]{:S(2)}) collective-permute-start(f32[64,128]{1,0:T(8,128)} %mine_ref.1), channel_id=1, source_target_pairs={{0,32},{32,0},{1,33},{33,1},{2,34},{34,2},{3,35},{35,3},{4,36},{36... | collective-permute-start | bytes 98312 | tf_op jit(solution)/shard_map/ppermute | solution.py:153
  17.8 0.8 copy-start.2
  18.6 24.4 %copy-start = (bf16[2048,384]{1,0:T(8,128)(2,1)S(1)}, bf16[2048,384]{1,0:T(8,128)(2,1)}, u32[]{:S(2)}) copy-start(bf16[2048,384]{1,0:T(8,128)(2,1)} %panel_ref.5) | copy-start | bytes 4718596
  18.6 24.4 %copy-start.1 = (f32[1024,384]{1,0:T(8,128)S(1)}, f32[1024,384]{1,0:T(8,128)}, u32[]{:S(2)}) copy-start(f32[1024,384]{1,0:T(8,128)} %param.7) | copy-start | bytes 4718596
  43.7 23.1 %all-to-all-start.2 = ((bf16[32,32,128]{2,1,0:T(8,128)(2,1)}), bf16[32,32,128]{2,1,0:T(8,128)(2,1)S(1)}, u32[]{:S(2)}, u32[]{:S(2)}) async-start(bf16[32,32,128]{2,1,0:T(8,128)(2,1)} %get-tuple-element.6), calls=%async_computation.2 | async-start | bytes 524288 | tf_op jit(solution)/shard_map/all_to_all | solution.py:170
  51.8 0.7 collective-permute-start.1
  88.9 6.3 %collective-permute-start.2 = (bf16[2,2,2,4,4,2,32,128]{7,6,5,4,3,2,1,0:T(8,128)(2,1)S(1)}, bf16[2,2,2,4,4,2,32,128]{7,6,5,4,3,2,1,0:T(8,128)(2,1)S(1)}, u32[]{:S(2)}, u32[]{:S(2)}) collective-permute-start(bf16[2,2,2,4,4,2,32,128]{7,6,5,4,3,2,1,0:T(8,128)(2,1)S(1)} %bitcast.7), channel_id=1, source_target_pairs={{0,32},{32,0},{1,33},{33,1},{2,34},{34,2},{3,35},{35,3},{4,36},{36... | collective-permute-start | bytes 6291464 | tf_op jit(solution)/shard_map/ppermute | solution.py:176

commit v5 on v4

--- a/solution.py
+++ b/solution.py
@@ -86,8 +86,8 @@
     )(shares, panel, trail)
 
 
-def stripes_kernel(core_ref, tiles_ref, panel_ref, trail_ref, *rest):
-    yn = pl.program_id(0) if tiles_ref.shape[0] > 1 else 0
+def stripes_kernel(core_ref, tiles_ref, panel_ref, trail_ref, passed_ref, out_ref, *rest):
+    yn = pl.program_id(0)
     _, near_z, _, far_y, far_z, far_x, _, _ = tiles_ref.shape
     rows = []
     for y in range(far_y):
@@ -99,30 +99,32 @@
         ]
         rows += [jnp.concatenate([p[h] for p in pairs], axis=1) for h in range(2)]
     update = jnp.dot(jnp.concatenate(rows, axis=0), panel_ref[...], preferred_element_type=jnp.float32)
-    out_ref = rest[-1]
-    out_ref[...] = trail_ref[...] - update.reshape(out_ref.shape)
+    out_ref[:, 0, 0] = trail_ref[:, yn, core_ref[0]] - update.reshape(far_y, -1, update.shape[1])
+    for solved_ref in rest:
+        solved_ref[...] = passed_ref[...]
 
 
-def updated_stripes(tiles, panel, trail, core, done=None):
+def updated_stripes(tiles, panel, trail, core, solved=None, done=None):
     near_y, far_y, height = tiles.shape[0], tiles.shape[3], tiles.shape[6]
     columns = panel.shape[1]
     stripe = pl.BlockSpec((far_y, 1, 1, 2 * height, columns), lambda i, core: (0, i, core[0], 0, 0))
     whole = pl.BlockSpec(memory_space=pltpu.VMEM)
-    one = pl.BlockSpec((1,) + tiles.shape[1:], lambda i, core: (i,) + (0,) * 7)
     flops = 2 * near_y * far_y * 2 * height * panel.shape[0] * columns
+    out = jax.ShapeDtypeStruct(trail.shape, jnp.float32)
+    block = None if solved is None else pl.BlockSpec(solved.shape, lambda i, core: (0, 0))
     return pl.pallas_call(
         stripes_kernel,
-        out_shape=jax.ShapeDtypeStruct(trail.shape, jnp.float32),
+        out_shape=out if solved is None else (out, jax.ShapeDtypeStruct(solved.shape, solved.dtype)),
         grid_spec=pltpu.PrefetchScalarGridSpec(
             num_scalar_prefetch=1,
             grid=(near_y,),
-            in_specs=[whole, whole, stripe] if done is None else [one, whole, stripe, pl.BlockSpec(memory_space=pl.ANY)],
-            out_specs=stripe,
+            in_specs=[whole, whole, whole, pl.BlockSpec(memory_space=pl.ANY) if solved is None else block],
+            out_specs=stripe if solved is None else (stripe, block),
         ),
-        input_output_aliases={} if done is None else {4: 0},
+        input_output_aliases={4: 0} if solved is None else {},
         compiler_params=vmem(20),
         cost_estimate=pl.CostEstimate(flops=flops, bytes_accessed=5 * 1024 * 1024, transcendentals=0),
-    )(core, tiles, panel, trail, *([] if done is None else [done]))
+    )(core, tiles, panel, trail, done if solved is None else solved)
 
 
 def cubes(size):
@@ -174,8 +176,8 @@
     )
     tiles = near.reshape(tuple(size[a] for a in NEAR + FAR) + far.shape[1:])
     other = lax.ppermute(tiles, "core", SWAP)
-    done = updated_stripes(tiles, panel, trail, core)
-    done = updated_stripes(other, panel, trail, 1 - core, done)
+    done, solved = updated_stripes(tiles, panel, trail, core, solved=solved)
+    done = updated_stripes(other, panel, trail, 1 - core, done=done)
     return solved, done.reshape(rhs_trail.shape)
 
 

time: 98.8 us -> 98.1 us (level)
  no operation moved by 1% of the time
where the time goes in v5:
time: 98.1 us; the launch traced here: 97.5 us
  blocking collectives  45.1 us (46%)
  starting transfers between devices  23.3 us (24%)
  waiting for transfers between devices  19.3 us (20%)
  Pallas kernels  6.43 us (7%)
  local copies, waits for them, and re-layouts  2.52 us (3%)
    all_to_all x1, blocking collectives, local(): shares = lax.all_to_all(blocks, COL, 0, 0, tiled=True)  23.3 us
    all_to_all x1, blocking collectives, local(): lax.all_to_all(jnp.broadcast_to(far[None], (copies,) + far.shape), ROW +...  21.7 us
    all_to_all x1, waiting for transfers between devices, local(): lax.all_to_all(low, FAR, 0, 0, tiled=True)  14.4 us
    all_to_all x1, starting transfers between devices, local(): lax.all_to_all(low, FAR, 0, 0, tiled=True)  8 us
    all_to_all x1, starting transfers between devices, local(): lax.all_to_all(jnp.broadcast_to(rows[None], (count_y,) + rows.shape), ('y...  7.65 us
    pallas_call x2, Pallas kernels, updated_stripes(): pl.pallas_call(stripes_kernel, out_shape=out if solved is None else (out,...  4.69 us
    ppermute x1, starting transfers between devices, local(): other_inverse = lax.ppermute(diag_inverse, 'core', SWAP)  4.52 us
    ppermute x1, starting transfers between devices, local(): other = lax.ppermute(tiles, 'core', SWAP)  2.49 us
  transfers between devices with their start and end apart: 5, of which 4 were waited for; matrix products, arithmetic and copies ran while one was open for 0% of the time, Pallas kernels for 2%

profile of v5, /device:TPU:1, one launch (start us, length us, event | category | flops | bytes accessed | tf_op | source)
XLA Modules:
  0.0 97.5 jit_solution(13590790866654526418)
XLA Ops:
  0.6 0.7 fusion
  1.4 0.1 pad_maximum_fusion
  1.4 0.7 broadcast_in_dim.4
  2.1 7.7 %all-to-all-start = ((f32[8,32,128]{2,1,0:T(8,128)}), f32[8,32,128]{2,1,0:T(8,128)S(1)}, u32[]{:S(2)}, u32[]{:S(2)}) async-start(f32[8,32,128]{2,1,0:T(8,128)} %broadcast_in_dim.4), calls=%async_computation | async-start | bytes 262144 | tf_op jit(solution)/shard_map/all_to_all | solution.py:158
  9.8 4.5 %collective-permute-start = (f32[64,128]{1,0:T(8,128)}, f32[64,128]{1,0:T(8,128)S(1)}, u32[]{:S(2)}, u32[]{:S(2)}) collective-permute-start(f32[64,128]{1,0:T(8,128)} %mine_ref.1), channel_id=1, source_target_pairs={{0,32},{32,0},{1,33},{33,1},{2,34},{34,2},{3,35},{35,3},{4,36},{36... | collective-permute-start | bytes 98312 | tf_op jit(solution)/shard_map/ppermute | solution.py:155
  14.3 1.0 %collective-permute-done.other_ref = f32[64,128]{1,0:T(8,128)S(1)} collective-permute-done((f32[64,128]{1,0:T(8,128)}, f32[64,128]{1,0:T(8,128)S(1)}, u32[]{:S(2)}, u32[]{:S(2)}) %collective-permute-start) | collective-permute-done | bytes 32800 | tf_op jit(solution)/shard_map/ppermute | solution.py:155
  15.3 2.5 %all-to-all-done.rhs_ref = f32[8,32,128]{2,1,0:T(8,128)S(1)} async-done(((f32[8,32,128]{2,1,0:T(8,128)}), f32[8,32,128]{2,1,0:T(8,128)S(1)}, u32[]{:S(2)}, u32[]{:S(2)}) %all-to-all-start) | async-done | bytes 131104 | tf_op jit(solution)/shard_map/all_to_all | solution.py:158
  17.8 0.0 copy-start.2
  17.8 0.8 copy-done.2
  18.6 1.0 shard_map.59
  19.6 23.3 %all_to_all.20 = f16[32,40,128]{2,1,0:T(8,128)(2,1)S(1)} all-to-all(f16[32,40,128]{2,1,0:T(8,128)(2,1)S(1)} %convert_element_type.6), channel_id=1, replica_groups=mesh['yf'=4,'yn'=2,'core'=2,'zf'=4,'zn'=2,'xf'=2,'xn'=2] {'zf','zn','xf'..., dimensions={0} | all-to-all | bytes 655360 | tf_op jit(solution)/shard_map/all_to_all | solution.py:160
  42.9 0.0 copy-done
  43.0 0.0 copy-done.1
  43.0 0.8 shard_map.60
  43.7 8.0 %all-to-all-start.2 = ((bf16[32,32,128]{2,1,0:T(8,128)(2,1)}), bf16[32,32,128]{2,1,0:T(8,128)(2,1)S(1)}, u32[]{:S(2)}, u32[]{:S(2)}) async-start(bf16[32,32,128]{2,1,0:T(8,128)(2,1)} %get-tuple-element.8), calls=%async_computation.2 | async-start | bytes 524288 | tf_op jit(solution)/shard_map/all_to_all | solution.py:172
  51.8 0.7 collective-permute-start.1
  52.4 0.0 collective-permute-done.1.passed_ref
  52.4 14.4 %all-to-all-done.2 = bf16[32,32,128]{2,1,0:T(8,128)(2,1)S(1)} async-done(((bf16[32,32,128]{2,1,0:T(8,128)(2,1)}), bf16[32,32,128]{2,1,0:T(8,128)(2,1)S(1)}, u32[]{:S(2)}, u32[]{:S(2)}) %all-to-all-start.2) | async-done | bytes 262176 | tf_op jit(solution)/shard_map/all_to_all | solution.py:172
  66.8 0.3 broadcast_in_dim.5
  67.2 21.7 %all_to_all.21 = bf16[8,32,32,128]{3,2,1,0:T(8,128)(2,1)S(1)} all-to-all(bf16[8,32,32,128]{3,2,1,0:T(8,128)(2,1)S(1)} %broadcast_in_dim.5), channel_id=1, replica_groups={{0,1,64,65,4,5,68,69},{2,3,66,67,6,7,70,71},{8,9,72,73,12,13,76,77},{10..., dimensions={0} | all-to-all | bytes 4194304 | tf_op jit(solution)/shard_map/all_to_all | solution.py:174
  88.9 2.5 %collective-permute-start.2 = (bf16[2,2,2,4,4,2,32,128]{7,6,5,4,3,2,1,0:T(8,128)(2,1)S(1)}, bf16[2,2,2,4,4,2,32,128]{7,6,5,4,3,2,1,0:T(8,128)(2,1)S(1)}, u32[]{:S(2)}, u32[]{:S(2)}) collective-permute-start(bf16[2,2,2,4,4,2,32,128]{7,6,5,4,3,2,1,0:T(8,128)(2,1)S(1)} %bitcast.7), channel_id=1, source_target_pairs={{0,32},{32,0},{1,33},{33,1},{2,34},{34,2},{3,35},{35,3},{4,36},{36... | collective-permute-start | bytes 6291464 | tf_op jit(solution)/shard_map/ppermute | solution.py:178
  91.4 2.4 %shard_map.61 = (f32[4,2,2,64,384]{4,3,2,1,0:T(8,128)}, f32[64,64]{1,0:T(8,128)}) custom-call(s32[1]{0:T(128)} %bitcast.core_ref, bf16[2,2,2,4,4,2,32,128]{7,6,5,4,3,2,1,0:T(8,128)(2,1)S(1)} %bitcast.8, bf16[2048,384]{1,0:T(8,128)(2,1)S(1)} %copy-done, f32[4,2,2,64,384]{4,3,2,1,0:T(8,128)S(1)} %bitcast.5, f32[64,64]{1,0:T(8,128)S(1)} %collective-permute-done.1.passed_ref), custom_call_target="tpu_custom_call" | custom-call | flops 805306368 | bytes 5242880 | tf_op jit(solution)/shard_map/pallas_call | solution.py:115
  93.7 1.4 %collective-permute-done.2.tiles_ref = bf16[2,2,2,4,4,2,32,128]{7,6,5,4,3,2,1,0:T(8,128)(2,1)S(1)} collective-permute-done((bf16[2,2,2,4,4,2,32,128]{7,6,5,4,3,2,1,0:T(8,128)(2,1)S(1)}, bf16[2,2,2,4,4,2,32,128]{7,6,5,4,3,2,1,0:T(8,128)(2,1)S(1)}, u32[]{:S(2)}, u32[]{:S(2)}) %collective-permute-start.2) | collective-permute-done | bytes 2097184 | tf_op jit(solution)/shard_map/ppermute | solution.py:178
  95.2 2.3 %shard_map.62 = f32[4,2,2,64,384]{4,3,2,1,0:T(8,128)} custom-call(s32[1]{0:T(128)S(6)} %sub.3.core_ref, bf16[2,2,2,4,4,2,32,128]{7,6,5,4,3,2,1,0:T(8,128)(2,1)S(1)} %collective-permute-done.2.tiles_ref, bf16[2048,384]{1,0:T(8,128)(2,1)S(1)} %copy-done, f32[4,2,2,64,384]{4,3,2,1,0:T(8,128)S(1)} %bitcast.6, ...), custom_call_target="tpu_custom_call", output_to_operand_aliasing={{}: (4, {})} | custom-call | flops 805306368 | bytes 5242880 | tf_op jit(solution)/shard_map/pallas_call | solution.py:115
  (4 shorter events, 0.1 us)
Async XLA Ops:
  2.1 15.7 %all-to-all-start = ((f32[8,32,128]{2,1,0:T(8,128)}), f32[8,32,128]{2,1,0:T(8,128)S(1)}, u32[]{:S(2)}, u32[]{:S(2)}) async-start(f32[8,32,128]{2,1,0:T(8,128)} %broadcast_in_dim.4), calls=%async_computation | async-start | bytes 262144 | tf_op jit(solution)/shard_map/all_to_all | solution.py:158
  9.8 5.6 %collective-permute-start = (f32[64,128]{1,0:T(8,128)}, f32[64,128]{1,0:T(8,128)S(1)}, u32[]{:S(2)}, u32[]{:S(2)}) collective-permute-start(f32[64,128]{1,0:T(8,128)} %mine_ref.1), channel_id=1, source_target_pairs={{0,32},{32,0},{1,33},{33,1},{2,34},{34,2},{3,35},{35,3},{4,36},{36... | collective-permute-start | bytes 98312 | tf_op jit(solution)/shard_map/ppermute | solution.py:155
  17.8 0.8 copy-start.2
  18.6 24.4 %copy-start = (bf16[2048,384]{1,0:T(8,128)(2,1)S(1)}, bf16[2048,384]{1,0:T(8,128)(2,1)}, u32[]{:S(2)}) copy-start(bf16[2048,384]{1,0:T(8,128)(2,1)} %panel_ref.5) | copy-start | bytes 4718596
  18.6 24.4 %copy-start.1 = (f32[1024,384]{1,0:T(8,128)S(1)}, f32[1024,384]{1,0:T(8,128)}, u32[]{:S(2)}) copy-start(f32[1024,384]{1,0:T(8,128)} %param.7) | copy-start | bytes 4718596
  43.7 23.1 %all-to-all-start.2 = ((bf16[32,32,128]{2,1,0:T(8,128)(2,1)}), bf16[32,32,128]{2,1,0:T(8,128)(2,1)S(1)}, u32[]{:S(2)}, u32[]{:S(2)}) async-start(bf16[32,32,128]{2,1,0:T(8,128)(2,1)} %get-tuple-element.8), calls=%async_computation.2 | async-start | bytes 524288 | tf_op jit(solution)/shard_map/all_to_all | solution.py:172
  51.8 0.7 collective-permute-start.1
  88.9 6.3 %collective-permute-start.2 = (bf16[2,2,2,4,4,2,32,128]{7,6,5,4,3,2,1,0:T(8,128)(2,1)S(1)}, bf16[2,2,2,4,4,2,32,128]{7,6,5,4,3,2,1,0:T(8,128)(2,1)S(1)}, u32[]{:S(2)}, u32[]{:S(2)}) collective-permute-start(bf16[2,2,2,4,4,2,32,128]{7,6,5,4,3,2,1,0:T(8,128)(2,1)S(1)} %bitcast.7), channel_id=1, source_target_pairs={{0,32},{32,0},{1,33},{33,1},{2,34},{34,2},{3,35},{35,3},{4,36},{36... | collective-permute-start | bytes 6291464 | tf_op jit(solution)/shard_map/ppermute | solution.py:178

commit v6 on v5

--- a/solution.py
+++ b/solution.py
@@ -64,13 +64,12 @@
 
 
 def sum_kernel(shares_ref, panel_ref, trail_ref, solved_ref, low_ref):
-    height, half = shares_ref.shape[1] - 8, shares_ref.shape[2] // 2
+    height = shares_ref.shape[1] - 8
     scale = jnp.exp2(shares_ref[:, height:] - TOP)
     total = jnp.concatenate(
         [jnp.sum(shares_ref[:, i : i + 8] * scale, axis=0) for i in range(0, height, 8)], axis=0
     )
-    solved_ref[:height] = total[:, :half]
-    solved_ref[height:] = pltpu.roll(total, half, 1)[:, :half]
+    solved_ref[...] = total
     low_ref[...] = jnp.broadcast_to(total.astype(jnp.bfloat16)[None], low_ref.shape)
 
 
@@ -79,7 +78,7 @@
     return pl.pallas_call(
         sum_kernel,
         out_shape=(
-            jax.ShapeDtypeStruct((2 * height, width // 2), jnp.float32),
+            jax.ShapeDtypeStruct((height, width), jnp.float32),
             jax.ShapeDtypeStruct((copies, height, width), jnp.bfloat16),
         ),
         compiler_params=vmem(8),
@@ -101,7 +100,9 @@
     update = jnp.dot(jnp.concatenate(rows, axis=0), panel_ref[...], preferred_element_type=jnp.float32)
     out_ref[:, 0, 0] = trail_ref[:, yn, core_ref[0]] - update.reshape(far_y, -1, update.shape[1])
     for solved_ref in rest:
-        solved_ref[...] = passed_ref[...]
+        both, (count, half) = passed_ref[...], passed_ref.shape
+        solved_ref[:count] = both[:, : half // 2]
+        solved_ref[count:] = pltpu.roll(both, half // 2, 1)[:, : half // 2]
 
 
 def updated_stripes(tiles, panel, trail, core, solved=None, done=None):
@@ -111,15 +112,17 @@
     whole = pl.BlockSpec(memory_space=pltpu.VMEM)
     flops = 2 * near_y * far_y * 2 * height * panel.shape[0] * columns
     out = jax.ShapeDtypeStruct(trail.shape, jnp.float32)
-    block = None if solved is None else pl.BlockSpec(solved.shape, lambda i, core: (0, 0))
+    if solved is not None:
+        tile = (2 * solved.shape[0], solved.shape[1] // 2)
+        block, unpacked = (pl.BlockSpec(shape, lambda i, core: (0, 0)) for shape in (solved.shape, tile))
     return pl.pallas_call(
         stripes_kernel,
-        out_shape=out if solved is None else (out, jax.ShapeDtypeStruct(solved.shape, solved.dtype)),
+        out_shape=out if solved is None else (out, jax.ShapeDtypeStruct(tile, solved.dtype)),
         grid_spec=pltpu.PrefetchScalarGridSpec(
             num_scalar_prefetch=1,
             grid=(near_y,),
             in_specs=[whole, whole, whole, pl.BlockSpec(memory_space=pl.ANY) if solved is None else block],
-            out_specs=stripe if solved is None else (stripe, block),
+            out_specs=stripe if solved is None else (stripe, unpacked),
         ),
         input_output_aliases={4: 0} if solved is None else {},
         compiler_params=vmem(20),
@@ -154,8 +157,9 @@
     core = lax.axis_index("core").reshape(1)
     other_inverse = lax.ppermute(diag_inverse, "core", SWAP)
     half, count_y, count_z = rhs_block.shape[0] // 2, size["yf"] * size["yn"], size["zf"] * size["zn"]
-    rows = jnp.concatenate([rhs_block[:half], rhs_block[half:]], axis=1)
-    rows = lax.all_to_all(jnp.broadcast_to(rows[None], (count_y,) + rows.shape), ("yf", "yn"), 0, 0, tiled=True)
+    shape = (count_y, half, rhs_block.shape[1])
+    rows = [jnp.broadcast_to(part[None], shape) for part in (rhs_block[:half], rhs_block[half:])]
+    rows = lax.all_to_all(jnp.concatenate(rows, axis=2), ("yf", "yn"), 0, 0, tiled=True)
     blocks = partial_blocks(rows, diag_inverse, other_inverse, core).astype(jnp.float16)
     shares = lax.all_to_all(blocks, COL, 0, 0, tiled=True)
     trail = rhs_trail.reshape(size["zf"], size["zn"], 2, 2 * half, rhs_trail.shape[1])

time: 98.1 us -> 98 us (level)
  no operation moved by 1% of the time
where the time goes in v6:
time: 98 us; the launch traced here: 97.3 us
  blocking collectives  45.1 us (46%)
  starting transfers between devices  22.9 us (23%)
  waiting for transfers between devices  19.4 us (20%)
  Pallas kernels  6.44 us (7%)
  local copies, waits for them, and re-layouts  1.88 us (2%)
    all_to_all x1, blocking collectives, local(): shares = lax.all_to_all(blocks, COL, 0, 0, tiled=True)  23.3 us
    all_to_all x1, blocking collectives, local(): lax.all_to_all(jnp.broadcast_to(far[None], (copies,) + far.shape), ROW +...  21.7 us
    all_to_all x1, waiting for transfers between devices, local(): lax.all_to_all(low, FAR, 0, 0, tiled=True)  14.4 us
    all_to_all x1, starting transfers between devices, local(): lax.all_to_all(low, FAR, 0, 0, tiled=True)  8.01 us
    all_to_all x1, starting transfers between devices, local(): lax.all_to_all(jnp.concatenate(rows, axis=2), ('yf', 'yn'), 0, 0, tiled=T...  7.65 us
    pallas_call x2, Pallas kernels, updated_stripes(): pl.pallas_call(stripes_kernel, out_shape=out if solved is None else (out,...  4.71 us
    ppermute x1, starting transfers between devices, local(): other_inverse = lax.ppermute(diag_inverse, 'core', SWAP)  4.52 us
    all_to_all x1, waiting for transfers between devices, local(): lax.all_to_all(jnp.concatenate(rows, axis=2), ('yf', 'yn'), 0, 0, tiled=T...  2.45 us
  transfers between devices with their start and end apart: 5, of which 4 were waited for; matrix products, arithmetic and copies ran while one was open for 0% of the time, Pallas kernels for 2%

profile of v6, /device:TPU:1, one launch (start us, length us, event | category | flops | bytes accessed | tf_op | source)
XLA Modules:
  0.0 97.3 jit_solution(1015672452864076059)
XLA Ops:
  0.6 0.7 fusion
  1.4 0.8 pad_maximum_fusion
  2.2 7.7 %all-to-all-start = ((f32[8,32,128]{2,1,0:T(8,128)}), f32[8,32,128]{2,1,0:T(8,128)S(1)}, u32[]{:S(2)}, u32[]{:S(2)}) async-start(f32[8,32,128]{2,1,0:T(8,128)} %pad_maximum_fusion), calls=%async_computation | async-start | bytes 262144 | tf_op jit(solution)/shard_map/all_to_all | solution.py:162
  9.8 4.5 %collective-permute-start = (f32[64,128]{1,0:T(8,128)}, f32[64,128]{1,0:T(8,128)S(1)}, u32[]{:S(2)}, u32[]{:S(2)}) collective-permute-start(f32[64,128]{1,0:T(8,128)} %mine_ref.1), channel_id=1, source_target_pairs={{0,32},{32,0},{1,33},{33,1},{2,34},{34,2},{3,35},{35,3},{4,36},{36... | collective-permute-start | bytes 98312 | tf_op jit(solution)/shard_map/ppermute | solution.py:158
  14.3 1.0 %collective-permute-done.other_ref = f32[64,128]{1,0:T(8,128)S(1)} collective-permute-done((f32[64,128]{1,0:T(8,128)}, f32[64,128]{1,0:T(8,128)S(1)}, u32[]{:S(2)}, u32[]{:S(2)}) %collective-permute-start) | collective-permute-done | bytes 32800 | tf_op jit(solution)/shard_map/ppermute | solution.py:158
  15.4 2.5 %all-to-all-done.rhs_ref = f32[8,32,128]{2,1,0:T(8,128)S(1)} async-done(((f32[8,32,128]{2,1,0:T(8,128)}), f32[8,32,128]{2,1,0:T(8,128)S(1)}, u32[]{:S(2)}, u32[]{:S(2)}) %all-to-all-start) | async-done | bytes 131104 | tf_op jit(solution)/shard_map/all_to_all | solution.py:162
  17.8 0.0 copy-start.2
  17.8 0.8 copy-done.2
  18.6 0.0 copy-start
  18.6 1.0 shard_map.59
  19.6 23.3 %all_to_all.20 = f16[32,40,128]{2,1,0:T(8,128)(2,1)S(1)} all-to-all(f16[32,40,128]{2,1,0:T(8,128)(2,1)S(1)} %convert_element_type.6), channel_id=1, replica_groups=mesh['yf'=4,'yn'=2,'core'=2,'zf'=4,'zn'=2,'xf'=2,'xn'=2] {'zf','zn','xf'..., dimensions={0} | all-to-all | bytes 655360 | tf_op jit(solution)/shard_map/all_to_all | solution.py:164
  43.0 0.0 copy-done
  43.0 0.0 copy-done.1
  43.0 0.8 shard_map.60
  43.8 8.0 %all-to-all-start.2 = ((bf16[32,32,128]{2,1,0:T(8,128)(2,1)}), bf16[32,32,128]{2,1,0:T(8,128)(2,1)S(1)}, u32[]{:S(2)}, u32[]{:S(2)}) async-start(bf16[32,32,128]{2,1,0:T(8,128)(2,1)} %get-tuple-element.8), calls=%async_computation.2 | async-start | bytes 524288 | tf_op jit(solution)/shard_map/all_to_all | solution.py:176
  51.8 0.7 collective-permute-start.1
  52.5 0.0 collective-permute-done.1.passed_ref
  52.5 14.4 %all-to-all-done.2 = bf16[32,32,128]{2,1,0:T(8,128)(2,1)S(1)} async-done(((bf16[32,32,128]{2,1,0:T(8,128)(2,1)}), bf16[32,32,128]{2,1,0:T(8,128)(2,1)S(1)}, u32[]{:S(2)}, u32[]{:S(2)}) %all-to-all-start.2) | async-done | bytes 262176 | tf_op jit(solution)/shard_map/all_to_all | solution.py:176
  66.9 0.3 broadcast_in_dim.8
  67.2 21.7 %all_to_all.21 = bf16[8,32,32,128]{3,2,1,0:T(8,128)(2,1)S(1)} all-to-all(bf16[8,32,32,128]{3,2,1,0:T(8,128)(2,1)S(1)} %broadcast_in_dim.8), channel_id=1, replica_groups={{0,1,64,65,4,5,68,69},{2,3,66,67,6,7,70,71},{8,9,72,73,12,13,76,77},{10..., dimensions={0} | all-to-all | bytes 4194304 | tf_op jit(solution)/shard_map/all_to_all | solution.py:178
  88.9 2.1 %collective-permute-start.2 = (bf16[2,2,2,4,4,2,32,128]{7,6,5,4,3,2,1,0:T(8,128)(2,1)S(1)}, bf16[2,2,2,4,4,2,32,128]{7,6,5,4,3,2,1,0:T(8,128)(2,1)S(1)}, u32[]{:S(2)}, u32[]{:S(2)}) collective-permute-start(bf16[2,2,2,4,4,2,32,128]{7,6,5,4,3,2,1,0:T(8,128)(2,1)S(1)} %bitcast.7), channel_id=1, source_target_pairs={{0,32},{32,0},{1,33},{33,1},{2,34},{34,2},{3,35},{35,3},{4,36},{36... | collective-permute-start | bytes 6291464 | tf_op jit(solution)/shard_map/ppermute | solution.py:182
  91.0 2.4 %shard_map.61 = (f32[4,2,2,64,384]{4,3,2,1,0:T(8,128)}, f32[64,64]{1,0:T(8,128)}) custom-call(s32[1]{0:T(128)} %bitcast.core_ref, bf16[2,2,2,4,4,2,32,128]{7,6,5,4,3,2,1,0:T(8,128)(2,1)S(1)} %bitcast.8, bf16[2048,384]{1,0:T(8,128)(2,1)S(1)} %copy-done, f32[4,2,2,64,384]{4,3,2,1,0:T(8,128)S(1)} %bitcast.5, f32[32,128]{1,0:T(8,128)S(1)} %collective-permute-done.1.passed_ref), custom_call_target="tpu_custom_call" | custom-call | flops 805306368 | bytes 5242880 | tf_op jit(solution)/shard_map/pallas_call | solution.py:118
  93.4 1.6 %collective-permute-done.2.tiles_ref = bf16[2,2,2,4,4,2,32,128]{7,6,5,4,3,2,1,0:T(8,128)(2,1)S(1)} collective-permute-done((bf16[2,2,2,4,4,2,32,128]{7,6,5,4,3,2,1,0:T(8,128)(2,1)S(1)}, bf16[2,2,2,4,4,2,32,128]{7,6,5,4,3,2,1,0:T(8,128)(2,1)S(1)}, u32[]{:S(2)}, u32[]{:S(2)}) %collective-permute-start.2) | collective-permute-done | bytes 2097184 | tf_op jit(solution)/shard_map/ppermute | solution.py:182
  95.0 2.3 %shard_map.62 = f32[4,2,2,64,384]{4,3,2,1,0:T(8,128)} custom-call(s32[1]{0:T(128)S(6)} %sub.3.core_ref, bf16[2,2,2,4,4,2,32,128]{7,6,5,4,3,2,1,0:T(8,128)(2,1)S(1)} %collective-permute-done.2.tiles_ref, bf16[2048,384]{1,0:T(8,128)(2,1)S(1)} %copy-done, f32[4,2,2,64,384]{4,3,2,1,0:T(8,128)S(1)} %bitcast.6, ...), custom_call_target="tpu_custom_call", output_to_operand_aliasing={{}: (4, {})} | custom-call | flops 805306368 | bytes 5242880 | tf_op jit(solution)/shard_map/pallas_call | solution.py:118
  (5 shorter events, 0.1 us)
Async XLA Ops:
  2.2 15.7 %all-to-all-start = ((f32[8,32,128]{2,1,0:T(8,128)}), f32[8,32,128]{2,1,0:T(8,128)S(1)}, u32[]{:S(2)}, u32[]{:S(2)}) async-start(f32[8,32,128]{2,1,0:T(8,128)} %pad_maximum_fusion), calls=%async_computation | async-start | bytes 262144 | tf_op jit(solution)/shard_map/all_to_all | solution.py:162
  9.8 5.6 %collective-permute-start = (f32[64,128]{1,0:T(8,128)}, f32[64,128]{1,0:T(8,128)S(1)}, u32[]{:S(2)}, u32[]{:S(2)}) collective-permute-start(f32[64,128]{1,0:T(8,128)} %mine_ref.1), channel_id=1, source_target_pairs={{0,32},{32,0},{1,33},{33,1},{2,34},{34,2},{3,35},{35,3},{4,36},{36... | collective-permute-start | bytes 98312 | tf_op jit(solution)/shard_map/ppermute | solution.py:158
  17.8 0.8 copy-start.2
  18.6 24.4 %copy-start = (bf16[2048,384]{1,0:T(8,128)(2,1)S(1)}, bf16[2048,384]{1,0:T(8,128)(2,1)}, u32[]{:S(2)}) copy-start(bf16[2048,384]{1,0:T(8,128)(2,1)} %panel_ref.5) | copy-start | bytes 4718596
  18.6 24.4 %copy-start.1 = (f32[1024,384]{1,0:T(8,128)S(1)}, f32[1024,384]{1,0:T(8,128)}, u32[]{:S(2)}) copy-start(f32[1024,384]{1,0:T(8,128)} %param.7) | copy-start | bytes 4718596
  43.8 23.1 %all-to-all-start.2 = ((bf16[32,32,128]{2,1,0:T(8,128)(2,1)}), bf16[32,32,128]{2,1,0:T(8,128)(2,1)S(1)}, u32[]{:S(2)}, u32[]{:S(2)}) async-start(bf16[32,32,128]{2,1,0:T(8,128)(2,1)} %get-tuple-element.8), calls=%async_computation.2 | async-start | bytes 524288 | tf_op jit(solution)/shard_map/all_to_all | solution.py:176
  51.8 0.7 collective-permute-start.1
  88.9 6.0 %collective-permute-start.2 = (bf16[2,2,2,4,4,2,32,128]{7,6,5,4,3,2,1,0:T(8,128)(2,1)S(1)}, bf16[2,2,2,4,4,2,32,128]{7,6,5,4,3,2,1,0:T(8,128)(2,1)S(1)}, u32[]{:S(2)}, u32[]{:S(2)}) collective-permute-start(bf16[2,2,2,4,4,2,32,128]{7,6,5,4,3,2,1,0:T(8,128)(2,1)S(1)} %bitcast.7), channel_id=1, source_target_pairs={{0,32},{32,0},{1,33},{33,1},{2,34},{34,2},{3,35},{35,3},{4,36},{36... | collective-permute-start | bytes 6291464 | tf_op jit(solution)/shard_map/ppermute | solution.py:182

commit v7 on v6

--- a/solution.py
+++ b/solution.py
@@ -28,14 +28,17 @@
     )
 
 
-def partial_kernel(rhs_ref, mine_ref, other_ref, core_ref, out_ref):
+def partial_kernel(rhs_ref, mine_ref, other_ref, core_ref, out_ref, here_ref, sem):
+    copy = pltpu.make_async_copy(mine_ref, here_ref, sem)
+    copy.start()
     count, height, half = rhs_ref.shape[0], rhs_ref.shape[1], rhs_ref.shape[2] // 2
     rows = []
     for i in range(count):
         both = rhs_ref[i]
         rows += [both[:, :half], pltpu.roll(both, half, 1)[:, :half]]
     first = core_ref[0] == 0
-    mine, other = mine_ref[...], other_ref[...]
+    copy.wait()
+    mine, other = here_ref[...], other_ref[...]
     inverse = jnp.concatenate([jnp.where(first, mine, other), jnp.where(first, other, mine)], axis=1)
     partial = jnp.dot(
         jnp.concatenate(rows, axis=0), inverse, preferred_element_type=jnp.float32, precision=lax.Precision.HIGHEST
@@ -58,7 +61,8 @@
     return pl.pallas_call(
         partial_kernel,
         out_shape=jax.ShapeDtypeStruct((count * 2 * mine.shape[1] // 64, height + 8, 128), jnp.float32),
-        in_specs=[whole, whole, whole, pl.BlockSpec(memory_space=pltpu.SMEM)],
+        in_specs=[whole, pl.BlockSpec(memory_space=pltpu.HBM), whole, pl.BlockSpec(memory_space=pltpu.SMEM)],
+        scratch_shapes=[pltpu.VMEM(mine.shape, mine.dtype), pltpu.SemaphoreType.DMA],
         compiler_params=vmem(8),
     )(rhs, mine, other, core)
 

time: 98 us -> 98.1 us (level)
  no operation moved by 1% of the time
where the time goes in v7:
time: 98.1 us; the launch traced here: 97.4 us
  blocking collectives  45.1 us (46%)
  starting transfers between devices  22.9 us (23%)
  waiting for transfers between devices  19.4 us (20%)
  Pallas kernels  6.53 us (7%)
  local copies, waits for them, and re-layouts  1.88 us (2%)
    all_to_all x1, blocking collectives, local(): shares = lax.all_to_all(blocks, COL, 0, 0, tiled=True)  23.3 us
    all_to_all x1, blocking collectives, local(): lax.all_to_all(jnp.broadcast_to(far[None], (copies,) + far.shape), ROW +...  21.7 us
    all_to_all x1, waiting for transfers between devices, local(): lax.all_to_all(low, FAR, 0, 0, tiled=True)  14.4 us
    all_to_all x1, starting transfers between devices, local(): lax.all_to_all(low, FAR, 0, 0, tiled=True)  8.01 us
    all_to_all x1, starting transfers between devices, local(): lax.all_to_all(jnp.concatenate(rows, axis=2), ('yf', 'yn'), 0, 0, tiled=T...  7.65 us
    pallas_call x2, Pallas kernels, updated_stripes(): pl.pallas_call(stripes_kernel, out_shape=out if solved is None else (out,...  4.71 us
    ppermute x1, starting transfers between devices, local(): other_inverse = lax.ppermute(diag_inverse, 'core', SWAP)  4.52 us
    all_to_all x1, waiting for transfers between devices, local(): lax.all_to_all(jnp.concatenate(rows, axis=2), ('yf', 'yn'), 0, 0, tiled=T...  2.45 us
  transfers between devices with their start and end apart: 5, of which 4 were waited for; matrix products, arithmetic and copies ran while one was open for 0% of the time, Pallas kernels for 2%

profile of v7, /device:TPU:1, one launch (start us, length us, event | category | flops | bytes accessed | tf_op | source)
XLA Modules:
  0.0 97.4 jit_solution(5925318985535824589)
XLA Ops:
  0.6 0.7 fusion
  1.4 0.8 pad_maximum_fusion
  2.2 7.7 %all-to-all-start = ((f32[8,32,128]{2,1,0:T(8,128)}), f32[8,32,128]{2,1,0:T(8,128)S(1)}, u32[]{:S(2)}, u32[]{:S(2)}) async-start(f32[8,32,128]{2,1,0:T(8,128)} %pad_maximum_fusion), calls=%async_computation | async-start | bytes 262144 | tf_op jit(solution)/shard_map/all_to_all | solution.py:166
  9.8 4.5 %collective-permute-start = (f32[64,128]{1,0:T(8,128)}, f32[64,128]{1,0:T(8,128)S(1)}, u32[]{:S(2)}, u32[]{:S(2)}) collective-permute-start(f32[64,128]{1,0:T(8,128)} %mine_ref.1), channel_id=1, source_target_pairs={{0,32},{32,0},{1,33},{33,1},{2,34},{34,2},{3,35},{35,3},{4,36},{36... | collective-permute-start | bytes 98312 | tf_op jit(solution)/shard_map/ppermute | solution.py:162
  14.3 1.0 %collective-permute-done.other_ref = f32[64,128]{1,0:T(8,128)S(1)} collective-permute-done((f32[64,128]{1,0:T(8,128)}, f32[64,128]{1,0:T(8,128)S(1)}, u32[]{:S(2)}, u32[]{:S(2)}) %collective-permute-start) | collective-permute-done | bytes 32800 | tf_op jit(solution)/shard_map/ppermute | solution.py:162
  15.4 2.5 %all-to-all-done.rhs_ref = f32[8,32,128]{2,1,0:T(8,128)S(1)} async-done(((f32[8,32,128]{2,1,0:T(8,128)}), f32[8,32,128]{2,1,0:T(8,128)S(1)}, u32[]{:S(2)}, u32[]{:S(2)}) %all-to-all-start) | async-done | bytes 131104 | tf_op jit(solution)/shard_map/all_to_all | solution.py:166
  17.8 0.0 copy-start.2
  17.8 0.8 copy-done.2
  18.6 0.0 copy-start
  18.6 1.0 %shard_map.59 = f32[32,40,128]{2,1,0:T(8,128)S(1)} custom-call(f32[8,32,128]{2,1,0:T(8,128)S(1)} %all-to-all-done.rhs_ref, f32[64,128]{1,0:T(8,128)S(1)} %copy-done.2, f32[64,128]{1,0:T(8,128)S(1)} %collective-permute-done.other_ref, s32[1]{0:T(128)} %bitcast.core_ref), custom_call_target="tpu_custom_call" | custom-call | tf_op jit(solution)/shard_map/pallas_call | solution.py:61
  19.7 23.3 %all_to_all.20 = f16[32,40,128]{2,1,0:T(8,128)(2,1)S(1)} all-to-all(f16[32,40,128]{2,1,0:T(8,128)(2,1)S(1)} %convert_element_type.6), channel_id=1, replica_groups=mesh['yf'=4,'yn'=2,'core'=2,'zf'=4,'zn'=2,'xf'=2,'xn'=2] {'zf','zn','xf'..., dimensions={0} | all-to-all | bytes 655360 | tf_op jit(solution)/shard_map/all_to_all | solution.py:168
  43.1 0.0 copy-done
  43.1 0.0 copy-done.1
  43.1 0.8 shard_map.60
  43.9 8.0 %all-to-all-start.2 = ((bf16[32,32,128]{2,1,0:T(8,128)(2,1)}), bf16[32,32,128]{2,1,0:T(8,128)(2,1)S(1)}, u32[]{:S(2)}, u32[]{:S(2)}) async-start(bf16[32,32,128]{2,1,0:T(8,128)(2,1)} %get-tuple-element.8), calls=%async_computation.2 | async-start | bytes 524288 | tf_op jit(solution)/shard_map/all_to_all | solution.py:180
  51.9 0.7 collective-permute-start.1
  52.6 0.0 collective-permute-done.1.passed_ref
  52.6 14.4 %all-to-all-done.2 = bf16[32,32,128]{2,1,0:T(8,128)(2,1)S(1)} async-done(((bf16[32,32,128]{2,1,0:T(8,128)(2,1)}), bf16[32,32,128]{2,1,0:T(8,128)(2,1)S(1)}, u32[]{:S(2)}, u32[]{:S(2)}) %all-to-all-start.2) | async-done | bytes 262176 | tf_op jit(solution)/shard_map/all_to_all | solution.py:180
  66.9 0.3 broadcast_in_dim.8
  67.3 21.7 %all_to_all.21 = bf16[8,32,32,128]{3,2,1,0:T(8,128)(2,1)S(1)} all-to-all(bf16[8,32,32,128]{3,2,1,0:T(8,128)(2,1)S(1)} %broadcast_in_dim.8), channel_id=1, replica_groups={{0,1,64,65,4,5,68,69},{2,3,66,67,6,7,70,71},{8,9,72,73,12,13,76,77},{10..., dimensions={0} | all-to-all | bytes 4194304 | tf_op jit(solution)/shard_map/all_to_all | solution.py:182
  89.0 2.1 %collective-permute-start.2 = (bf16[2,2,2,4,4,2,32,128]{7,6,5,4,3,2,1,0:T(8,128)(2,1)S(1)}, bf16[2,2,2,4,4,2,32,128]{7,6,5,4,3,2,1,0:T(8,128)(2,1)S(1)}, u32[]{:S(2)}, u32[]{:S(2)}) collective-permute-start(bf16[2,2,2,4,4,2,32,128]{7,6,5,4,3,2,1,0:T(8,128)(2,1)S(1)} %bitcast.7), channel_id=1, source_target_pairs={{0,32},{32,0},{1,33},{33,1},{2,34},{34,2},{3,35},{35,3},{4,36},{36... | collective-permute-start | bytes 6291464 | tf_op jit(solution)/shard_map/ppermute | solution.py:186
  91.1 2.4 %shard_map.61 = (f32[4,2,2,64,384]{4,3,2,1,0:T(8,128)}, f32[64,64]{1,0:T(8,128)}) custom-call(s32[1]{0:T(128)} %bitcast.core_ref, bf16[2,2,2,4,4,2,32,128]{7,6,5,4,3,2,1,0:T(8,128)(2,1)S(1)} %bitcast.8, bf16[2048,384]{1,0:T(8,128)(2,1)S(1)} %copy-done, f32[4,2,2,64,384]{4,3,2,1,0:T(8,128)S(1)} %bitcast.5, f32[32,128]{1,0:T(8,128)S(1)} %collective-permute-done.1.passed_ref), custom_call_target="tpu_custom_call" | custom-call | flops 805306368 | bytes 5242880 | tf_op jit(solution)/shard_map/pallas_call | solution.py:122
  93.5 1.6 %collective-permute-done.2.tiles_ref = bf16[2,2,2,4,4,2,32,128]{7,6,5,4,3,2,1,0:T(8,128)(2,1)S(1)} collective-permute-done((bf16[2,2,2,4,4,2,32,128]{7,6,5,4,3,2,1,0:T(8,128)(2,1)S(1)}, bf16[2,2,2,4,4,2,32,128]{7,6,5,4,3,2,1,0:T(8,128)(2,1)S(1)}, u32[]{:S(2)}, u32[]{:S(2)}) %collective-permute-start.2) | collective-permute-done | bytes 2097184 | tf_op jit(solution)/shard_map/ppermute | solution.py:186
  95.1 2.3 %shard_map.62 = f32[4,2,2,64,384]{4,3,2,1,0:T(8,128)} custom-call(s32[1]{0:T(128)S(6)} %sub.3.core_ref, bf16[2,2,2,4,4,2,32,128]{7,6,5,4,3,2,1,0:T(8,128)(2,1)S(1)} %collective-permute-done.2.tiles_ref, bf16[2048,384]{1,0:T(8,128)(2,1)S(1)} %copy-done, f32[4,2,2,64,384]{4,3,2,1,0:T(8,128)S(1)} %bitcast.6, ...), custom_call_target="tpu_custom_call", output_to_operand_aliasing={{}: (4, {})} | custom-call | flops 805306368 | bytes 5242880 | tf_op jit(solution)/shard_map/pallas_call | solution.py:122
  (5 shorter events, 0.1 us)
Async XLA Ops:
  2.2 15.7 %all-to-all-start = ((f32[8,32,128]{2,1,0:T(8,128)}), f32[8,32,128]{2,1,0:T(8,128)S(1)}, u32[]{:S(2)}, u32[]{:S(2)}) async-start(f32[8,32,128]{2,1,0:T(8,128)} %pad_maximum_fusion), calls=%async_computation | async-start | bytes 262144 | tf_op jit(solution)/shard_map/all_to_all | solution.py:166
  9.8 5.6 %collective-permute-start = (f32[64,128]{1,0:T(8,128)}, f32[64,128]{1,0:T(8,128)S(1)}, u32[]{:S(2)}, u32[]{:S(2)}) collective-permute-start(f32[64,128]{1,0:T(8,128)} %mine_ref.1), channel_id=1, source_target_pairs={{0,32},{32,0},{1,33},{33,1},{2,34},{34,2},{3,35},{35,3},{4,36},{36... | collective-permute-start | bytes 98312 | tf_op jit(solution)/shard_map/ppermute | solution.py:162
  17.8 0.8 copy-start.2
  18.6 24.5 %copy-start = (bf16[2048,384]{1,0:T(8,128)(2,1)S(1)}, bf16[2048,384]{1,0:T(8,128)(2,1)}, u32[]{:S(2)}) copy-start(bf16[2048,384]{1,0:T(8,128)(2,1)} %panel_ref.5) | copy-start | bytes 4718596
  18.6 24.5 %copy-start.1 = (f32[1024,384]{1,0:T(8,128)S(1)}, f32[1024,384]{1,0:T(8,128)}, u32[]{:S(2)}) copy-start(f32[1024,384]{1,0:T(8,128)} %param.7) | copy-start | bytes 4718596
  43.9 23.1 %all-to-all-start.2 = ((bf16[32,32,128]{2,1,0:T(8,128)(2,1)}), bf16[32,32,128]{2,1,0:T(8,128)(2,1)S(1)}, u32[]{:S(2)}, u32[]{:S(2)}) async-start(bf16[32,32,128]{2,1,0:T(8,128)(2,1)} %get-tuple-element.8), calls=%async_computation.2 | async-start | bytes 524288 | tf_op jit(solution)/shard_map/all_to_all | solution.py:180
  51.9 0.7 collective-permute-start.1
  89.0 6.0 %collective-permute-start.2 = (bf16[2,2,2,4,4,2,32,128]{7,6,5,4,3,2,1,0:T(8,128)(2,1)S(1)}, bf16[2,2,2,4,4,2,32,128]{7,6,5,4,3,2,1,0:T(8,128)(2,1)S(1)}, u32[]{:S(2)}, u32[]{:S(2)}) collective-permute-start(bf16[2,2,2,4,4,2,32,128]{7,6,5,4,3,2,1,0:T(8,128)(2,1)S(1)} %bitcast.7), channel_id=1, source_target_pairs={{0,32},{32,0},{1,33},{33,1},{2,34},{34,2},{3,35},{35,3},{4,36},{36... | collective-permute-start | bytes 6291464 | tf_op jit(solution)/shard_map/ppermute | solution.py:186
